TPU v7x, 256 devices: a whole 4x4x8 slice. The times are simulated.
256 devices in a mesh: ctx: 16 (over x_lo, z), head: 8 (over y, core), dp: 2 (over x_hi).
Axes of the slice: x: 4 (x_hi: 2, x_lo: 2; x = x_hi * 2 + x_lo), y: 4, z: 8, core: 2. Of those that a mesh axis runs over, the one named last changes fastest.
Arguments:
- inputs: bfloat16 [2, 16384, 4096], P('dp', 'ctx', 'head'), may hold values from -6 to 6
- q_base: bfloat16 [2, 16384, 4096], P('dp', 'ctx', 'head'), may hold values from -20 to 20
- k_base: bfloat16 [2, 16384, 4096], P('dp', 'ctx', 'head'), may hold values from -20 to 20
- v_base: bfloat16 [2, 16384, 4096], P('dp', 'ctx', 'head'), may hold values from -6 to 6
- d_out: bfloat16 [2, 16384, 4096], P('dp', 'ctx', 'head'), may hold values from -0.1796875 to 0.1796875
- d_ctx_base: bfloat16 [2, 16384, 4096], P('dp', 'ctx', 'head'), may hold values from -0.1796875 to 0.1796875
- flags: int32 [32], P('head'), may hold values from 0 to 1, as said below
- query_down_factor: bfloat16 [16, 4096], P(None, 'head'), may hold values from -0.09375 to 0.09375
- up_q: bfloat16 [16, 4096], P(None, 'head'), may hold values from -0.29882812 to 0.29882812
- key_down_factor: bfloat16 [16, 4096], P(None, 'head'), may hold values from -0.09375 to 0.09375
- up_k: bfloat16 [16, 4096], P(None, 'head'), may hold values from -0.29882812 to 0.29882812
- value_down_factor: bfloat16 [16, 4096], P(None, 'head'), may hold values from -0.09375 to 0.09375
- up_v: bfloat16 [16, 4096], P(None, 'head'), may hold values from -0.29882812 to 0.29882812
- down_o: bfloat16 [16, 4096], P(None, 'head'), may hold values from -0.09375 to 0.09375
- output_up_factor: bfloat16 [16, 4096], P(None, 'head'), may hold values from -0.29882812 to 0.29882812
Outputs:
- query_down_gradient: float32 [16, 4096], P(None, 'head')
- query_up_gradient: float32 [16, 4096], P(None, 'head')
- key_down_gradient: float32 [16, 4096], P(None, 'head')
- key_up_gradient: float32 [16, 4096], P(None, 'head')
- value_down_gradient: float32 [16, 4096], P(None, 'head')
- value_up_gradient: float32 [16, 4096], P(None, 'head')
- output_down_gradient: float32 [16, 4096], P(None, 'head')
- output_up_gradient: float32 [16, 4096], P(None, 'head')
Inputs may be any that keep to these rules, and one draw needn't show every extreme that they name: `flags`: in every aligned block of 4 heads exactly half are 1.
All inputs are finite; a program needn't handle non-finite values.
Results may differ from a plain program's by a relative error of at most 0.012.
The roundings to bfloat16 on the way count: a program that leaves them out, or rounds other values in their place, can miss the bound.
Values may be sent and summed in bfloat16 or wider, within the bound.
A program may use at most 128 MiB of HBM per device.

v0:
```python
import math

import jax
import jax.numpy as jnp
from jax import lax
from jax.sharding import PartitionSpec as P

HD = 128
GROUP = 1024
SHIFT = 512


adapter_scale = 2.0


def from_behind(value, axis, steps):
    count = lax.axis_size(axis)
    pairs = [(source, (source + steps) % count) for source in range(count)]
    return lax.ppermute(value, axis, pairs)


def exact_product(left_operand, right_operand):
    return jnp.dot(
        left_operand,
        right_operand,
        precision=lax.Precision.HIGHEST,
        preferred_element_type=jnp.float32,
    )


def group_attention(block):
    scale = 1.0 / math.sqrt(HD)
    total = block.shape[1]
    count = total // GROUP
    query = block[0].reshape(count, GROUP, HD)
    keys = block[1].reshape(count, GROUP, HD)
    values = block[2].reshape(count, GROUP, HD)
    upstream = block[3].reshape(count, GROUP, HD)
    scores = jnp.einsum("gqd,gkd->gqk", query, keys, preferred_element_type=jnp.float32) * scale
    causal = lax.broadcasted_iota(jnp.int32, (GROUP, GROUP), 0) >= lax.broadcasted_iota(
        jnp.int32, (GROUP, GROUP), 1
    )
    scores = jnp.where(causal, scores, -jnp.inf)
    peak = jnp.max(scores, axis=-1, keepdims=True)
    weights = jnp.exp(scores - peak)
    probs = weights / jnp.sum(weights, axis=-1, keepdims=True)
    probs_low = probs.astype(jnp.bfloat16)
    context = jnp.einsum(
        "gqk,gkd->gqd", probs_low, values, preferred_element_type=jnp.float32
    ).astype(jnp.bfloat16)
    grad_probs = jnp.einsum("gqd,gkd->gqk", upstream, values, preferred_element_type=jnp.float32)
    center = jnp.sum(probs * grad_probs, axis=-1, keepdims=True)
    grad_scores = (probs * (grad_probs - center) * scale).astype(jnp.bfloat16)
    grad_query = jnp.einsum("gqk,gkd->gqd", grad_scores, keys, preferred_element_type=jnp.float32)
    grad_keys = jnp.einsum("gqk,gqd->gkd", grad_scores, query, preferred_element_type=jnp.float32)
    grad_values = jnp.einsum(
        "gqk,gqd->gkd", probs_low, upstream, preferred_element_type=jnp.float32
    )
    grads = jnp.stack([grad_query, grad_keys, grad_values]).reshape(3, total, HD)
    return (context.reshape(total, HD), grads)


def attend_heads(stacked):
    per_head = jnp.moveaxis(stacked, 2, 0)
    context, grads = lax.map(group_attention, per_head)
    return (jnp.moveaxis(context, 0, 1), jnp.moveaxis(grads, 0, 2))


def on_device(
    inputs,
    q_base,
    k_base,
    v_base,
    d_out,
    d_ctx_base,
    flags,
    query_down_factor,
    up_q,
    key_down_factor,
    up_k,
    value_down_factor,
    up_v,
    down_o,
    output_up_factor,
):
    feature_rows = inputs[0]
    output_gradient = d_out[0]
    rows = feature_rows.shape[0]
    heads = flags.shape[0]
    half = heads // 2
    rank = query_down_factor.shape[0]
    keep = rows - SHIFT
    terms = jnp.concatenate(
        [
            jnp.dot(feature_rows, query_down_factor.T, preferred_element_type=jnp.float32),
            jnp.dot(feature_rows, key_down_factor.T, preferred_element_type=jnp.float32),
            jnp.dot(feature_rows, value_down_factor.T, preferred_element_type=jnp.float32),
            jnp.dot(output_gradient, output_up_factor.T, preferred_element_type=jnp.float32),
        ],
        axis=1,
    )
    latents = lax.psum(terms, "head")
    lat_query = latents[:, :rank]
    lat_keys = latents[:, rank : 2 * rank]
    lat_values = latents[:, 2 * rank : 3 * rank]
    combined_gradient = latents[:, 3 * rank :]

    def adapted(frozen_output, latent_rows, upper_factor):
        return (
            frozen_output[0].astype(jnp.float32)
            + adapter_scale * exact_product(latent_rows, upper_factor.astype(jnp.float32))
        ).astype(jnp.bfloat16)

    stacked = jnp.stack(
        [
            adapted(q_base, lat_query, up_q),
            adapted(k_base, lat_keys, up_k),
            adapted(v_base, lat_values, up_v),
            adapted(d_ctx_base, combined_gradient, down_o),
        ]
    )
    stacked = stacked.reshape(4, rows, heads, HD)
    order = jnp.argsort(1 - flags, stable=True)
    inverse = jnp.argsort(order, stable=True)
    moved = jnp.take(stacked, order[:half], axis=2)
    staying = jnp.take(stacked, order[half:], axis=2)
    arriving = from_behind(moved[:, :SHIFT], "ctx", -1)
    rolled = jnp.concatenate([moved[:, SHIFT:], arriving], axis=1)
    context, grads = attend_heads(jnp.concatenate([rolled, staying], axis=2))
    ctx_moved = context[:, :half]
    grads_moved = grads[:, :, :half]
    ctx_tail = ctx_moved[keep:]
    grads_tail = grads_moved[:, keep:]

    def restore(moved_part, staying_part):
        return jnp.take(jnp.concatenate([moved_part, staying_part], axis=-2), inverse, axis=-2)

    package = jnp.concatenate([grads_tail, ctx_tail.astype(jnp.float32)[None]], axis=0)
    returned = from_behind(package, "ctx", 1)
    grads_own = jnp.concatenate([returned[:3], grads_moved[:, :keep]], axis=1)
    ctx_own = jnp.concatenate([returned[3].astype(jnp.bfloat16), ctx_moved[:keep]], axis=0)
    grads_full = restore(grads_own, grads[:, :, half:]).reshape(3, rows, heads * HD)
    ctx_full = restore(ctx_own, context[:, half:]).reshape(rows, heads * HD)
    partial_value = jnp.concatenate(
        [
            exact_product(grads_full[0], up_q.astype(jnp.float32).T),
            exact_product(grads_full[1], up_k.astype(jnp.float32).T),
            exact_product(grads_full[2], up_v.astype(jnp.float32).T),
            jnp.dot(ctx_full, down_o.T, preferred_element_type=jnp.float32),
        ],
        axis=1,
    )
    extra_up = [0.0, 0.0, 0.0]
    extra_down = 0.0
    sums = lax.psum(partial_value, "head")
    feats_wide = feature_rows.astype(jnp.float32)
    query_down_gradient = exact_product(sums[:, :rank].T, feats_wide)
    key_down_gradient = exact_product(sums[:, rank : 2 * rank].T, feats_wide)
    value_down_gradient = exact_product(sums[:, 2 * rank : 3 * rank].T, feats_wide)
    output_up_gradient = exact_product(sums[:, 3 * rank :].T, output_gradient.astype(jnp.float32))
    query_up_gradient = exact_product(lat_query.T, grads_full[0]) + extra_up[0]
    key_up_gradient = exact_product(lat_keys.T, grads_full[1]) + extra_up[1]
    value_up_gradient = exact_product(lat_values.T, grads_full[2]) + extra_up[2]
    output_down_gradient = (
        exact_product(combined_gradient.T, ctx_full.astype(jnp.float32)) + extra_down
    )
    return lax.psum(
        (
            adapter_scale * query_down_gradient,
            adapter_scale * query_up_gradient,
            adapter_scale * key_down_gradient,
            adapter_scale * key_up_gradient,
            adapter_scale * value_down_gradient,
            adapter_scale * value_up_gradient,
            adapter_scale * output_down_gradient,
            adapter_scale * output_up_gradient,
        ),
        ("ctx", "dp"),
    )


def solution(mesh):
    placed = (
        P("dp", "ctx", "head"),
        P("dp", "ctx", "head"),
        P("dp", "ctx", "head"),
        P("dp", "ctx", "head"),
        P("dp", "ctx", "head"),
        P("dp", "ctx", "head"),
        P("head"),
        P(None, "head"),
        P(None, "head"),
        P(None, "head"),
        P(None, "head"),
        P(None, "head"),
        P(None, "head"),
        P(None, "head"),
        P(None, "head"),
    )
    return jax.shard_map(
        on_device,
        mesh=mesh,
        in_specs=placed,
        out_specs=(
            P(None, "head"),
            P(None, "head"),
            P(None, "head"),
            P(None, "head"),
            P(None, "head"),
            P(None, "head"),
            P(None, "head"),
            P(None, "head"),
        ),
        check_vma=False,
    )
```

profile of v0, /device:TPU:1, one launch (start us, length us, event | category | flops | bytes accessed | tf_op | source)
XLA Modules:
  0.0 526.9 jit_solution(14766040172759266743)
XLA Ops:
  20.7 60.4 %all-reduce.5.cloned.1.call-done = f32[1024,64]{0,1:T(8,128)} async-done(((f32[1024,64]{0,1:T(8,128)}), f32[1024,64]{0,1:T(8,128)}) %all-reduce.5.cloned.1.call-update) | async-done | bytes 262160 | tf_op jit(solution)/shard_map/psum | solution.py:102
  81.0 3.4 fusion.18
  84.4 2.2 copy.44
  86.7 3.3 fusion.19
  90.0 2.3 copy.43
  92.3 2.1 fusion.20
  94.4 2.3 copy.42
  98.4 3.7 pad_maximum_fusion.1
  102.1 3.1 gather_fusion.2
  106.9 3.9 collective-permute-start
  110.9 3.1 gather_fusion.3
  114.3 16.6 %collective-permute-done = bf16[4,512,2,128]{3,1,0,2:T(8,128)(2,1)} collective-permute-done((bf16[4,512,2,128]{3,1,0,2:T(8,128)(2,1)}, bf16[4,512,2,128]{3,1,0,2:T(8,128)(2,1)}, u32[]{:S(2)}, u32[]{:S(2)}) %collective-permute-start) | collective-permute-done | bytes 1048608 | tf_op jit(solution)/shard_map/ppermute | solution.py:19
  130.9 3.5 maximum_bitcast_fusion.1
  134.4 62.1 %while.12 = (s32[]{:T(128)}, bf16[4,1024,128]{2,1,0:T(8,128)(2,1)S(1)}, f32[4,3,1024,128]{3,2,0,1:T(8,128)}, bf16[4,4,1024,128]{3,2,1,0:T(8,128)(2,1)}, s32[]{:T(128)}, /*index=5*/s32[]{:T(128)}, s32[]{}, s32[]{}, s32[]{}) while((s32[]{:T(128)}, bf16[4,1024,128]{2,1,0:T(8,128)(2,1)S(1)}, f32[4,3,1024,128]{3,2,0,1:T(8,128)}, ...), condition=%wide.region_7.9_spmd, body=%wide.region_3.8_spmd.sunk | while | flops 1650324480 | bytes 80536800 | solution.py:65
  136.7 2.1 fusion.91
  138.8 3.1 convolution_bitcast_fusion.6
  142.3 1.9 multiply_reduce_fusion.2
  152.2 2.1 fusion.91
  154.3 3.1 convolution_bitcast_fusion.6
  167.8 2.1 fusion.91
  169.9 3.1 convolution_bitcast_fusion.6
  173.4 1.9 multiply_reduce_fusion.2
  183.3 2.1 fusion.91
  185.4 3.1 convolution_bitcast_fusion.6
  188.9 1.9 multiply_reduce_fusion.2
  197.5 2.1 fusion.49
  203.1 3.8 slice.139
  206.9 41.1 %collective-permute-done.1 = f32[4,512,2,128]{3,1,2,0:T(8,128)} collective-permute-done((f32[4,512,2,128]{3,1,2,0:T(8,128)}, f32[4,512,2,128]{3,1,2,0:T(8,128)}, u32[]{:S(2)}, u32[]{:S(2)}) %collective-permute-start.1) | collective-permute-done | bytes 2097184 | tf_op jit(solution)/shard_map/ppermute | solution.py:19
  250.2 2.9 gather_fusion.1
  253.1 2.3 copy.49
  259.7 3.1 pad_maximum_fusion
  262.8 6.4 %gather_fusion = f32[4,3,1024,128]{3,2,1,0:T(8,128)} fusion(f32[3,1024,4,128]{3,1,2,0:T(8,128)} %pad_maximum_fusion, s32[1024]{0:T(1024)S(1)} %pad_clamp_fusion), kind=kCustom, calls=%fused_computation.2 | custom fusion | bytes 12582928 | tf_op jit(solution)/shard_map/jit(_take)/gather | solution.py:136
  269.2 3.4 select_bitcast_fusion
  272.6 2.8 fusion.48
  275.4 1.9 copy.48
  278.2 2.9 copy.47
  281.1 3.0 fusion.52
  284.1 2.9 copy.46
  287.0 2.4 fusion.51
  291.3 4.1 convolution_multiply_fusion.6
  295.4 4.0 convolution_multiply_fusion.4
  299.4 2.5 convolution_multiply_fusion.2
  303.4 55.7 %all-reduce.7.cloned.1.call-done = f32[1024,64]{0,1:T(8,128)} async-done(((f32[1024,64]{0,1:T(8,128)}), f32[1024,64]{0,1:T(8,128)}) %all-reduce.7.cloned.1.call-update) | async-done | bytes 262160 | tf_op jit(solution)/shard_map/psum | solution.py:155
  359.1 2.0 convolution_multiply_fusion.7
  361.1 2.0 convolution_multiply_fusion.5
  363.0 2.0 convolution_multiply_fusion.3
  365.0 2.4 convolution_multiply_fusion
  367.4 142.0 %all-reduce.9.cloned.1.call-done = (f32[16,512]{1,0:T(8,128)}, f32[16,512]{1,0:T(8,128)}, f32[16,512]{1,0:T(8,128)}, f32[16,512]{1,0:T(8,128)}, f32[16,512]{1,0:...) async-done(((f32[16,512]{1,0:T(8,128)}, f32[16,512]{1,0:T(8,128)}, f32[16,512]{1,0:T(8,128)}, f32[16,512]{1,0:T(8,128)}, f32[16,512]{1,0:T(8,128)}, ...) | async-done | bytes 262160 | tf_op jit(solution)/shard_map/psum | solution.py:167
  (136 shorter events, 78.8 us)
Async XLA Ops:
  7.2 1.2 copy-start
  7.2 6.9 %copy-start.22 = (s32[4]{0:T(128)S(1)}, s32[4]{0:T(128)}, u32[]{:S(2)}) copy-start(s32[4]{0:T(128)} %param.25) | copy-start | bytes 52
  7.2 7.8 %copy-start.9 = (bf16[1,1024,512]{2,1,0:T(8,128)(2,1)S(1)}, bf16[1,1024,512]{2,1,0:T(8,128)(2,1)}, u32[]{:S(2)}) copy-start(bf16[1,1024,512]{2,1,0:T(8,128)(2,1)} %param.24) | copy-start | bytes 3145732
  7.2 9.1 %copy-start.10 = (bf16[1,1024,512]{2,1,0:T(8,128)(2,1)S(1)}, bf16[1,1024,512]{2,1,0:T(8,128)(2,1)}, u32[]{:S(2)}) copy-start(bf16[1,1024,512]{2,1,0:T(8,128)(2,1)} %param.22) | copy-start | bytes 3145732
  7.2 73.8 %all-reduce.5.cloned.1.call-start = ((), (), s32[]{:S(2)}) async-start(), calls=%async_computation | async-start | bytes 524288 | tf_op jit(solution)/shard_map/psum | solution.py:102
  14.1 345.0 %all-reduce.7.cloned.1.call-start = ((), (), s32[]{:S(2)}) async-start(), calls=%async_computation.1 | async-start | bytes 524288 | tf_op jit(solution)/shard_map/psum | solution.py:155
  14.9 5.7 %copy-start.20 = (s32[4]{0:T(128)}, s32[4]{0:T(128)S(1)}, u32[]{:S(2)}) copy-start(s32[4]{0:T(128)S(1)} %get-tuple-element.34) | copy-start | bytes 52
  15.0 66.0 %copy-start.13 = (bf16[16,512]{1,0:T(8,128)(2,1)S(1)}, bf16[16,512]{1,0:T(8,128)(2,1)}, u32[]{:S(2)}) copy-start(bf16[16,512]{1,0:T(8,128)(2,1)} %param.32) | copy-start | bytes 49156
  17.6 69.0 %copy-start.15 = (bf16[16,512]{1,0:T(8,128)(2,1)S(1)}, bf16[16,512]{1,0:T(8,128)(2,1)}, u32[]{:S(2)}) copy-start(bf16[16,512]{1,0:T(8,128)(2,1)} %param.31) | copy-start | bytes 49156
  20.6 71.6 %copy-start.17 = (bf16[16,512]{1,0:T(8,128)(2,1)S(1)}, bf16[16,512]{1,0:T(8,128)(2,1)}, u32[]{:S(2)}) copy-start(bf16[16,512]{1,0:T(8,128)(2,1)} %param.29) | copy-start | bytes 49156
  81.0 5.7 %copy-start.7 = (f32[1024,64]{0,1:T(8,128)S(1)}, f32[1024,64]{0,1:T(8,128)}, u32[]{:S(2)}) copy-start(f32[1024,64]{0,1:T(8,128)} %all-reduce.5.cloned.1.call-done) | copy-start | bytes 786436
  86.7 10.0 %copy-start.19 = (bf16[16,512]{1,0:T(8,128)(2,1)S(1)}, bf16[16,512]{1,0:T(8,128)(2,1)}, u32[]{:S(2)}) copy-start(bf16[16,512]{1,0:T(8,128)(2,1)} %param.27) | copy-start | bytes 49156
  106.9 23.9 %collective-permute-start = (bf16[4,512,2,128]{3,1,0,2:T(8,128)(2,1)}, bf16[4,512,2,128]{3,1,0,2:T(8,128)(2,1)}, u32[]{:S(2)}, u32[]{:S(2)}) collective-permute-start(bf16[4,512,2,128]{3,1,0,2:T(8,128)(2,1)} %get-tuple-element.68), channel_id=1, source_target_pairs={{0,240},{16,0},{32,16},{48,32},{64,48},{80,64},{96,80},{112,96},{1... | collective-permute-start | bytes 3145736 | tf_op jit(solution)/shard_map/ppermute | solution.py:19
  114.0 16.9 %copy-start.6 = (bf16[4,512,2,128]{3,1,0,2:T(8,128)(2,1)S(1)}, bf16[4,512,2,128]{3,1,0,2:T(8,128)(2,1)}, u32[]{:S(2)}) copy-start(bf16[4,512,2,128]{3,1,0,2:T(8,128)(2,1)} %get-tuple-element.67) | copy-start | bytes 3145732
  130.9 3.5 copy-start.11
  136.2 2.6 copy-start.1
  138.8 3.5 copy-start.2
  151.7 2.6 copy-start.1
  154.3 3.5 copy-start.2
  167.2 2.6 copy-start.1
  169.9 3.5 copy-start.2
  182.8 2.6 copy-start.1
  185.4 3.5 copy-start.2
  196.5 1.0 copy-start.12
  197.5 3.7 copy-start.21
  201.2 46.9 %collective-permute-start.1 = (f32[4,512,2,128]{3,1,2,0:T(8,128)}, f32[4,512,2,128]{3,1,2,0:T(8,128)}, u32[]{:S(2)}, u32[]{:S(2)}) collective-permute-start(f32[4,512,2,128]{3,1,2,0:T(8,128)} %pad_maximum_fusion.2), channel_id=1, source_target_pairs={{0,16},{16,32},{32,48},{48,64},{64,80},{80,96},{96,112},{112,128},... | collective-permute-start | bytes 6291464 | tf_op jit(solution)/shard_map/ppermute | solution.py:19
  249.1 8.8 %copy-start.14 = (bf16[16,512]{1,0:T(8,128)(2,1)S(1)}, bf16[16,512]{1,0:T(8,128)(2,1)}, u32[]{:S(2)}) copy-start(bf16[16,512]{1,0:T(8,128)(2,1)} %param.32) | copy-start | bytes 49156
  255.4 4.4 copy-start.3
  256.9 1.1 copy-start.4
  275.4 2.0 copy-start.16
  277.3 3.7 copy-start.18
  281.1 10.2 %copy-start.8 = (f32[1024,64]{0,1:T(8,128)S(1)}, f32[1024,64]{0,1:T(8,128)}, u32[]{:S(2)}) copy-start(f32[1024,64]{0,1:T(8,128)} %all-reduce.5.cloned.1.call-done) | copy-start | bytes 786436
  291.0 218.4 %all-reduce.9.cloned.1.call-start = ((), (), s32[]{:S(2)}) async-start(), calls=%async_computation.2 | async-start | bytes 524288 | tf_op jit(solution)/shard_map/psum | solution.py:167
  291.3 10.6 %copy-start.5 = (bf16[1024,512]{0,1:T(8,128)(2,1)S(1)}, bf16[1024,512]{0,1:T(8,128)(2,1)}, u32[]{:S(2)}) copy-start(bf16[1024,512]{0,1:T(8,128)(2,1)} %copy-done.4) | copy-start | bytes 3145732
Sparse Core Ops, SparseCore 0:
  14.2 66.7 all-reduce.4
  291.1 67.9 all-reduce.6
  367.6 141.8 all-reduce.8
where the time goes:
time: 533 us; the launch traced here: 527 us
  waiting for transfers between devices  316 us (59%)
  matrix products  90.5 us (17%)
  local copies, waits for them, and re-layouts  68.4 us (13%)
  other arithmetic  33.7 us (6%)
  between operations  14 us (3%)
    psum x1, waiting for transfers between devices, on_device(): lax.psum((adapter_scale * query_down_gradient, adapter_scale * query_up_g...  142 us
    psum x1, waiting for transfers between devices, on_device(): latents = lax.psum(terms, 'head')  60.4 us
    ppermute x2, waiting for transfers between devices, from_behind(): return lax.ppermute(value, axis, pairs)  57.7 us
    psum x1, waiting for transfers between devices, on_device(): sums = lax.psum(partial_value, 'head')  55.7 us
    dot_general x15, matrix products, exact_product(): jnp.dot(left_operand, right_operand, precision=lax.Precision.HIGHEST, pre...  36.6 us
    unnamed x54, local copies, waits for them, and re-layouts  19.8 us
    dot_general x4, matrix products, group_attention(): jnp.einsum('gqk,gqd->gkd', probs_low, upstream, preferred_element_type=jn...  12.4 us
    gather x3, local copies, waits for them, and re-layouts, restore(): jnp.take(jnp.concatenate([moved_part, staying_part], axis=-2), inverse, a...  11.5 us
  transfers between devices with their start and end apart: 5, of which 5 were waited for; matrix products, arithmetic and copies ran while one was open for 5% of the time, Pallas kernels for 0%

commit v1 on v0

v1 whole, which is shorter than its diff:
```python
import functools
import math

import jax
import jax.numpy as jnp
from jax import lax
from jax.experimental import pallas as pl
from jax.experimental.pallas import tpu as pltpu
from jax.sharding import PartitionSpec as P

HD = 128
ROWS = 1024
HALF = 512
CHUNK = 256
RANK = 16
WIDTH = 512
NY, NZ, NX = 4, 8, 4
SCALE = 1.0 / math.sqrt(HD)
EXP_SCALE = SCALE * math.log2(math.e)
MESH = pl.DeviceIdType.MESH
F32 = jnp.float32
BF16 = jnp.bfloat16
NN = (((1,), (0,)), ((), ()))
NT = (((1,), (1,)), ((), ()))


def dot(a, b, dims=NN):
    return lax.dot_general(a, b, dims, preferred_element_type=F32)


def place(block):
    return (block // 2) % 2 * 4 + block % 2 + 2 * (block // 4)


def split_rows(wide, kinds):
    rows = []
    for t in range(kinds):
        part = wide[RANK * t : RANK * (t + 1)]
        high = part.astype(BF16).astype(F32)
        rows += [high, part - high]
    return jnp.concatenate(rows, axis=0)


def fold(pair):
    return pair[:RANK] + pair[RANK:]


def chunk_scores(keys, values, keys_t, values_t, query, upstream):
    length = keys.shape[0]
    scores = dot(keys, query, NT)
    own = scores[length - CHUNK :]
    causal = lax.broadcasted_iota(jnp.int32, own.shape, 0) <= lax.broadcasted_iota(
        jnp.int32, own.shape, 1
    )
    own = jnp.where(causal, own, -jnp.inf)
    scores = own if length == CHUNK else jnp.concatenate([scores[: length - CHUNK], own], axis=0)
    peak = jnp.max(scores, axis=0, keepdims=True)
    weights = jnp.exp2((scores - peak) * EXP_SCALE)
    probs = weights * (1.0 / jnp.sum(weights, axis=0, keepdims=True))
    grad_probs = dot(values, upstream, NT)
    center = jnp.sum(probs * grad_probs, axis=0, keepdims=True)
    grad_scores = (probs * (grad_probs - center) * SCALE).astype(BF16)
    probs_low = probs.astype(BF16)
    context_t = dot(values_t, probs_low)
    grad_query_t = dot(keys_t, grad_scores)
    return probs_low, grad_scores, context_t.astype(BF16), grad_query_t.astype(BF16)


def kernel(
    x_hbm, q_hbm, k_hbm, v_hbm, do_hbm, dc_hbm, flags,
    down_q, up_q, down_k, up_k, down_v, up_v, down_o, up_o,
    out_ref,
    xb, qb, kb, vb, dob, dcb,
    kv_stage, kv_in,
    part, sib_in, acc, y_in, total,
    lat_prev, up_pad, fac, prev_up, lat_low, prev_low, prev_cols,
    qa, ka, va, ua, kt, vt,
    grads, back, back_in, up_sum,
    cut, x_in, x_sum, z_in, z_all, x_all,
    load_sem, kv_send, kv_recv, lp_send, lp_recv, back_send, back_recv,
    sib_send, sib_recv, y1_send, y1_recv, y2_send, y2_recv, fw_send, fw_recv,
    x1_send, x1_recv, z1_send, z1_recv, z2_send, z2_recv, x2_send, x2_recv,
):
    ctx, head, dp = lax.axis_index("ctx"), lax.axis_index("head"), lax.axis_index("dp")
    y, core = head // 2, head % 2
    x_lo, z = ctx // NZ, ctx % NZ
    x = dp * 2 + x_lo
    sibling = {"head": y * 2 + (1 - core)}
    after = lax.rem(ctx + 1, 2 * NZ)
    before = lax.rem(ctx + 2 * NZ - 1, 2 * NZ)

    def y_peer(d):
        return {"head": lax.rem(y + d, NY) * 2 + core}

    def z_peer(d):
        return {"ctx": x_lo * NZ + lax.rem(z + d, NZ)}

    def x_peer(d):
        other = lax.rem(x + d, NX)
        return {"ctx": (other % 2) * NZ + z, "dp": other // 2}

    loads = []
    pairs = [(x_hbm, xb), (do_hbm, dob)]
    for source, target in ((k_hbm, kb), (v_hbm, vb), (q_hbm, qb), (dc_hbm, dcb)):
        pairs += [(source.at[:, pl.ds(HD * h, HD)], target.at[h]) for h in range(4)]
    for i, (source, target) in enumerate(pairs):
        copy = pltpu.make_async_copy(source, target, load_sem.at[i])
        copy.start()
        loads.append(copy)

    barrier = pltpu.get_barrier_semaphore()
    peers = [sibling]
    peers += [y_peer(d) for d in range(1, NY)]
    peers += [z_peer(d) for d in range(1, NZ)]
    peers += [x_peer(d) for d in range(1, NX)]
    for near in (after, before):
        peers += [{"ctx": near}, {"ctx": near, "head": y * 2 + (1 - core)}]
    for peer in peers:
        pl.semaphore_signal(barrier, inc=1, device_id=peer, device_id_type=MESH)

    sends = []

    def remote(source, target, send_sem, recv_sem, peer):
        return pltpu.make_async_remote_copy(
            src_ref=source, dst_ref=target, send_sem=send_sem, recv_sem=recv_sem,
            device_id=peer, device_id_type=MESH,
        )

    def send(*args):
        copy = remote(*args)
        copy.start()
        sends.append(copy)

    f0, f1, f2, f3 = (flags[h] for h in range(4))
    head_of = (
        (1 - f0) * (2 - f1),
        3 * f3 + (1 - f3) * (1 + f2),
        f0 * (1 + f1),
        3 * (1 - f3) + f3 * (2 - f2),
    )
    slot_of = (
        2 - 2 * f0,
        f1 * f0 + (1 - f1) * (2 + 1 - f0),
        f2 * (f0 + f1) + (1 - f2) * (4 - f0 - f1),
        f3 + (1 - f3) * 3,
    )

    up_pad[...] = jnp.zeros_like(up_pad)
    for t, factor in enumerate((up_q, up_k, up_v, down_o)):
        for copy_at in (0, RANK):
            up_pad[32 * t + copy_at : 32 * t + copy_at + RANK, WIDTH * t : WIDTH * (t + 1)] = factor[...]
        for h in range(4):
            fac[t, h] = factor[:, HD * h : HD * (h + 1)]
    for t in range(2):
        for h in range(4):
            at = WIDTH * (1 + t) + HD * h
            prev_up[t, h] = up_pad[32:96, at : at + HD]
    grads[...] = jnp.zeros_like(grads)
    back[...] = jnp.zeros_like(back)
    up_sum[...] = jnp.zeros_like(up_sum)

    loads[0].wait()
    first = jnp.concatenate([down_q[...], down_k[...], down_v[...]], axis=0)
    lat_part = dot(first, xb[...], NT)
    loads[1].wait()
    mix_part = dot(up_o[...], dob[...], NT)
    for b in range(8):
        part[0, place(b), :48] = lat_part[:, HD * b : HD * (b + 1)]
        part[0, place(b), 48:] = mix_part[:, HD * b : HD * (b + 1)]

    pl.semaphore_wait(barrier, len(peers))

    def sum_heads(p, late=None):
        mine = core * 4
        other = (1 - core) * 4
        send(part.at[p, pl.ds(other, 4)], sib_in.at[p], sib_send.at[p], sib_recv.at[p], sibling)
        yield
        remote(part.at[p, pl.ds(other, 4)], sib_in.at[p], sib_send.at[p], sib_recv.at[p], sibling).wait_recv()
        for i in range(4):
            acc[p, i] = part[p, mine + i] + sib_in[p, i]
        if late is not None:
            late()
        for d in range(1, NY):
            send(acc.at[p, lax.rem(y + d, NY)], y_in.at[p, d - 1], y1_send.at[p, d - 1], y1_recv.at[p, d - 1], y_peer(d))
        yield
        for d in range(1, NY):
            remote(acc.at[p, 0], y_in.at[p, d - 1], y1_send.at[p, d - 1], y1_recv.at[p, d - 1], y_peer(d)).wait_recv()
        own = total.at[p, mine + y]
        own[...] = acc[p, y] + y_in[p, 0] + y_in[p, 1] + y_in[p, 2]
        for d in range(1, NY):
            send(own, own, y2_send.at[p, d - 1], y2_recv.at[p, d - 1], y_peer(d))
        send(own, own, fw_send.at[p, 0], fw_recv.at[p, 0], sibling)
        yield
        for d in range(1, NY):
            came = total.at[p, mine + lax.rem(y + NY - d, NY)]
            remote(came, came, y2_send.at[p, d - 1], y2_recv.at[p, d - 1], y_peer(d)).wait_recv()
            send(came, came, fw_send.at[p, d], fw_recv.at[p, d], sibling)
        yield
        for d in range(NY):
            came = total.at[p, other + lax.rem(y + NY - d, NY)]
            remote(came, came, fw_send.at[p, d], fw_recv.at[p, d], sibling).wait_recv()
        yield

    def sum_tokens(e):
        for d in range(1, NX):
            send(cut.at[e, lax.rem(x + d, NX)], x_in.at[e, d - 1], x1_send.at[e, d - 1], x1_recv.at[e, d - 1], x_peer(d))
        yield
        for d in range(1, NX):
            remote(cut.at[e, 0], x_in.at[e, d - 1], x1_send.at[e, d - 1], x1_recv.at[e, d - 1], x_peer(d)).wait_recv()
        x_sum[e] = cut[e, x] + x_in[e, 0] + x_in[e, 1] + x_in[e, 2]
        for d in range(1, NZ):
            send(x_sum.at[e, lax.rem(z + d, NZ)], z_in.at[e, d - 1], z1_send.at[e, d - 1], z1_recv.at[e, d - 1], z_peer(d))
        yield
        for d in range(1, NZ):
            remote(x_sum.at[e, 0], z_in.at[e, d - 1], z1_send.at[e, d - 1], z1_recv.at[e, d - 1], z_peer(d)).wait_recv()
        own = z_all.at[e, z]
        summed = x_sum[e, z]
        for d in range(1, NZ):
            summed = summed + z_in[e, d - 1]
        own[...] = summed
        for d in range(1, NZ):
            send(own, own, z2_send.at[e, d - 1], z2_recv.at[e, d - 1], z_peer(d))
        yield
        for d in range(1, NZ):
            came = z_all.at[e, lax.rem(z + NZ - d, NZ)]
            remote(came, came, z2_send.at[e, d - 1], z2_recv.at[e, d - 1], z_peer(d)).wait_recv()
        for d in range(1, NX):
            send(z_all.at[e], x_all.at[e, x], x2_send.at[e, d - 1], x2_recv.at[e, d - 1], x_peer(d))
        x_all[e, x] = z_all[e]
        yield
        for d in range(1, NX):
            came = x_all.at[e, lax.rem(x + NX - d, NX)]
            remote(z_all.at[e], came, x2_send.at[e, d - 1], x2_recv.at[e, d - 1], x_peer(d)).wait_recv()
        for c in range(4):
            for r in range(8):
                out_ref[e, 8 * r : 8 * r + 8, HD * c : HD * (c + 1)] = x_all[e, c, r]
        yield

    latents = sum_heads(0)
    next(latents)

    for copy in loads[2:10]:
        copy.wait()
    for s in range(2):
        for i, base in enumerate((kb, vb)):
            kv_stage[s, i] = base[head_of[s], HALF:, :]
        send(kv_stage.at[s], kv_in.at[s], kv_send.at[s], kv_recv.at[s], {"ctx": after})

    for _ in range(4):
        next(latents)

    for c in range(2):
        send(
            total.at[0, pl.ds(4 * c + 2, 2), pl.ds(RANK, 2 * RANK)], lat_prev.at[pl.ds(2 * c, 2)],
            lp_send.at[c], lp_recv.at[c], {"ctx": after},
        )
    for copy in loads[10:]:
        copy.wait()

    def adapt(b, carry):
        rows = pl.ds(pl.multiple_of(b * HD, HD), HD)
        both = split_rows(2.0 * total[0, place(b)], 4)
        lat_low[:, rows] = both.astype(BF16)
        extra = dot(both.T.astype(BF16), up_pad[...])
        for t, (base, full, turned) in enumerate(
            ((qb, qa, None), (kb, ka, kt), (vb, va, vt), (dcb, ua, None))
        ):
            for h in range(4):
                at = WIDTH * t + HD * h
                low = (base[h, rows, :].astype(F32) + extra[:, at : at + HD]).astype(BF16)
                full[h, rows, :] = low
                if turned is not None:
                    turned[h, :, rows] = low.T
        return carry

    lax.fori_loop(0, 8, adapt, 0)

    for c in range(2):
        remote(
            total.at[0, pl.ds(4 * c + 2, 2), pl.ds(RANK, 2 * RANK)], lat_prev.at[pl.ds(2 * c, 2)],
            lp_send.at[c], lp_recv.at[c], {"ctx": after},
        ).wait_recv()
    for b in range(4):
        both = split_rows(2.0 * lat_prev[b], 2)
        prev_low[:, HD * b : HD * (b + 1)] = both.astype(BF16)
        prev_cols[HD * b : HD * (b + 1), :] = both.T.astype(BF16)

    def attend(slot, h, first_at, off):
        last_at = HALF - first_at
        uq, uk, uv, od = (fac[t, h] for t in range(4))
        off_k, off_v, off_kt, off_vt = off if off is not None else (
            ka[h, :HALF, :], va[h, :HALF, :], kt[h, :, :HALF], vt[h, :, :HALF],
        )
        sums = [0.0, 0.0, 0.0, 0.0]

        def keys_done(t, factor, grad, lat, put):
            low = grad.astype(BF16)
            put(t, dot(factor, low, NT))
            sums[t] = sums[t] + fold(dot(lat, low))

        def queries_done(t, factor, grad_t, lat, put):
            put(t, dot(factor, grad_t))
            sums[t] = sums[t] + fold(dot(lat, grad_t, NT))

        def lat_of(t, at):
            return lat_low[32 * t : 32 * t + 32, at : at + HALF]

        def put_at(at):
            def put(t, value):
                grads[RANK * t : RANK * (t + 1), at : at + HALF] += value
            return put

        def put_back(t, value):
            for b in range(4):
                back[b // 2, b % 2, RANK * (t - 1) : RANK * t] += value[:, HD * b : HD * (b + 1)]

        for at, with_off in ((first_at, False), (last_at, True)):
            own = slice(at, at + HALF)
            keys, values = ka[h, own, :], va[h, own, :]
            keys_t, values_t = kt[h, :, own], vt[h, :, own]
            query, upstream = qa[h, own, :], ua[h, own, :]
            ahead = 0
            if with_off:
                ahead = HALF
                keys = jnp.concatenate([off_k, keys], axis=0)
                values = jnp.concatenate([off_v, values], axis=0)
                keys_t = jnp.concatenate([off_kt, keys_t], axis=1)
                values_t = jnp.concatenate([off_vt, values_t], axis=1)
            results = []
            for c in range(2):
                length = ahead + CHUNK * (c + 1)
                here = slice(CHUNK * c, CHUNK * (c + 1))
                results.append(
                    chunk_scores(
                        keys[:length], values[:length], keys_t[:, :length], values_t[:, :length],
                        query[here], upstream[here],
                    )
                )
            short = ahead + CHUNK
            (p0, s0, c0, q0), (p1, s1, c1, q1) = results

            def over_queries(early, late, rows):
                return jnp.concatenate(
                    [
                        dot(early, rows[:CHUNK]) + dot(late[:short], rows[CHUNK:]),
                        dot(late[short:], rows[CHUNK:]),
                    ],
                    axis=0,
                )

            grad_keys = over_queries(s0, s1, query)
            grad_values = over_queries(p0, p1, upstream)
            queries_done(0, uq, jnp.concatenate([q0, q1], axis=1), lat_of(0, at), put_at(at))
            queries_done(3, od, jnp.concatenate([c0, c1], axis=1), lat_of(3, at), put_at(at))
            for t, factor, grad in ((1, uk, grad_keys), (2, uv, grad_values)):
                keys_done(t, factor, grad[ahead:], lat_of(t, at), put_at(at))
                if with_off and off is None:
                    keys_done(t, factor, grad[:ahead], lat_of(t, 0), put_at(0))
                elif with_off:
                    keys_done(t, factor, grad[:ahead], prev_low[32 * t - 32 : 32 * t, :], put_back)
        for t in range(4):
            up_sum[slot, RANK * t : RANK * (t + 1)] = sums[t]

    def back_copy(c):
        return remote(
            back.at[c], back_in.at[core], back_send.at[c], back_recv.at[core],
            {"ctx": before, "head": y * 2 + c},
        )

    def both_kinds(i, carry):
        h = head_of[0] + i * (head_of[1] - head_of[0])
        still = head_of[2] + i * (head_of[3] - head_of[2])
        remote(kv_stage.at[i], kv_in.at[i], kv_send.at[i], kv_recv.at[i], {"ctx": after}).wait_recv()
        off_k = (kv_in[i, 0].astype(F32) + dot(prev_cols[...], prev_up[0, h])).astype(BF16)
        off_v = (kv_in[i, 1].astype(F32) + dot(prev_cols[...], prev_up[1, h])).astype(BF16)
        attend(i, h, HALF, (off_k, off_v, off_k.T, off_v.T))

        @pl.when(i == 1)
        def _():
            for c in range(2):
                back_copy(c).start()

        attend(2 + i, still, 0, None)
        return carry

    lax.fori_loop(0, 2, both_kinds, 0)

    for b in range(8):
        part[1, place(b)] = grads[:, HD * b : HD * (b + 1)]

    def add_back():
        for c in range(2):
            remote(back.at[c], back_in.at[c], back_send.at[c], back_recv.at[c], sibling).wait_recv()
        for i in range(2):
            acc[1, 2 + i, RANK : 3 * RANK] += back_in[0, i] + back_in[1, i]

    shares = sum_heads(1, add_back)
    next(shares)
    for h in range(4):
        piece = up_sum[jnp.minimum(slot_of[h], 3)]
        for r in range(8):
            cut[0, h, r] = piece[8 * r : 8 * r + 8]
    ups = sum_tokens(0)
    next(ups)
    next(shares)
    next(ups)
    next(shares)
    next(ups)
    next(shares)
    next(shares)

    wide = []
    for b in range(8):
        wide.append(split_rows(2.0 * total[1, place(b)], 4).astype(BF16))
    wide = jnp.concatenate(wide, axis=1)
    down = dot(wide[:96], xb[...])
    last = fold(dot(wide[96:], dob[...]))
    down = jnp.concatenate([fold(down[32 * t : 32 * t + 32]) for t in range(3)] + [last], axis=0)
    for c in range(4):
        for r in range(8):
            cut[1, c, r] = down[8 * r : 8 * r + 8, HD * c : HD * (c + 1)]
    downs = sum_tokens(1)
    next(downs)
    next(ups)
    next(downs)
    next(downs)
    next(ups)
    next(downs)
    next(downs)
    for copy in sends:
        copy.wait_send()
    for c in range(2):
        back_copy(c).wait_send()


def on_device(
    inputs, q_base, k_base, v_base, d_out, d_ctx_base, flags,
    query_down_factor, up_q, key_down_factor, up_k, value_down_factor, up_v, down_o, output_up_factor,
):
    anywhere = pl.BlockSpec(memory_space=pl.ANY)
    vmem = pl.BlockSpec(memory_space=pltpu.VMEM)
    smem = pl.BlockSpec(memory_space=pltpu.SMEM)
    dma = pltpu.SemaphoreType.DMA
    v = pltpu.VMEM
    out = pl.pallas_call(
        kernel,
        out_shape=jax.ShapeDtypeStruct((2, 64, WIDTH), F32),
        in_specs=[anywhere] * 6 + [smem] + [vmem] * 8,
        out_specs=vmem,
        scratch_shapes=[
            *[v((ROWS, WIDTH), BF16) for _ in range(1)], *[v((4, ROWS, HD), BF16) for _ in range(3)],
            v((ROWS, WIDTH), BF16), v((4, ROWS, HD), BF16),
            v((2, 2, HALF, HD), BF16), v((2, 2, HALF, HD), BF16),
            v((2, 8, 64, HD), F32), v((2, 4, 64, HD), F32), v((2, 4, 64, HD), F32),
            v((2, 3, 64, HD), F32), v((2, 8, 64, HD), F32),
            v((4, 32, HD), F32), v((128, 4 * WIDTH), BF16), v((4, 4, RANK, HD), BF16),
            v((2, 4, 64, HD), BF16), v((128, ROWS), BF16),
            v((64, HALF), BF16), v((HALF, 64), BF16),
            *[v((4, ROWS, HD), BF16) for _ in range(4)],
            *[v((4, HD, ROWS), BF16) for _ in range(2)],
            v((64, ROWS), F32), v((2, 2, 32, HD), F32), v((2, 2, 32, HD), F32), v((4, 64, HD), F32),
            v((2, 4, 8, 8, HD), F32), v((2, 3, 8, 8, HD), F32), v((2, 8, 8, HD), F32),
            v((2, 7, 8, HD), F32), v((2, 8, 8, HD), F32), v((2, 4, 8, 8, HD), F32),
            dma((18,)), dma((2,)), dma((2,)), dma((2,)), dma((2,)), dma((2,)), dma((2,)),
            dma((2,)), dma((2,)), dma((2, 3)), dma((2, 3)), dma((2, 3)), dma((2, 3)), dma((2, 4)), dma((2, 4)),
            dma((2, 3)), dma((2, 3)), dma((2, 7)), dma((2, 7)), dma((2, 7)), dma((2, 7)), dma((2, 3)), dma((2, 3)),
        ],
        compiler_params=pltpu.CompilerParams(
            collective_id=0, has_side_effects=True, vmem_limit_bytes=56 * 1024 * 1024
        ),
    )(
        inputs[0], q_base[0], k_base[0], v_base[0], d_out[0], d_ctx_base[0], flags,
        query_down_factor, up_q, key_down_factor, up_k, value_down_factor, up_v, down_o, output_up_factor,
    )
    result = []
    for t in range(4):
        rows = slice(RANK * t, RANK * (t + 1))
        result += [out[1, rows], out[0, rows]]
    return (result[0], result[1], result[2], result[3], result[4], result[5], result[7], result[6])


def solution(mesh):
    tokens = P("dp", "ctx", "head")
    factor = P(None, "head")
    return jax.shard_map(
        on_device,
        mesh=mesh,
        in_specs=(tokens,) * 6 + (P("head"),) + (factor,) * 8,
        out_specs=(factor,) * 8,
        check_vma=False,
    )
```

time: 533 us -> 72.4 us (0.14)
  waiting for transfers between devices: 316 us -> 0 us
  matrix products: 90.5 us -> 0 us
  Pallas kernels: 0 us -> 68.9 us
  local copies, waits for them, and re-layouts: 68.4 us -> 1.57 us
  other arithmetic: 33.7 us -> 0 us
  between operations: 14 us -> 0.65 us
    psum x3 -> x0, waiting for transfers between devices: 258 us -> none  [the longest x1 142 us: on_device(): lax.psum((adapter_scale * query_down_gradient, adapter_scale * query_up_g...]
    dot_general x44 -> x0, matrix products: 90.5 us -> none  [the longest x15 36.6 us: exact_product(): jnp.dot(left_operand, right_operand, precision=lax.Precision.HIGHEST, pre...]
    pallas_call x0 -> x1, Pallas kernels: none -> 68.9 us  [on_device(): pl.pallas_call(kernel, out_shape=jax.ShapeDtypeStruct((2, 64, WIDTH), F32...]
    ppermute x2 -> x0, waiting for transfers between devices: 57.7 us -> none  [from_behind(): return lax.ppermute(value, axis, pairs)]
    slice x9 -> x0, local copies, waits for them, and re-layouts: 20.5 us -> none  [the longest x2 5.7 us: on_device(): grads_full[0]]
    unnamed x54 -> x0, local copies, waits for them, and re-layouts: 19.8 us -> none
    gather x5 -> x0, local copies, waits for them, and re-layouts: 17.8 us -> none  [the longest x3 11.5 us: restore(): jnp.take(jnp.concatenate([moved_part, staying_part], axis=-2), inverse, a...]
    concatenate x5 -> x0, other arithmetic: 8.03 us -> none  [the longest x2 4.16 us: restore(): jnp.concatenate([moved_part, staying_part], axis=-2)]
  transfers between devices with their start and end apart: 5 -> 0, of which waited for: 5 -> 0; matrix products, arithmetic and copies ran while one was open for 5% -> 0% of each run, Pallas kernels for 0% -> 0%
where the time goes in v1:
time: 72.4 us; the launch traced here: 71.2 us
  Pallas kernels  68.9 us (95%)
  local copies, waits for them, and re-layouts  1.57 us (2%)
    pallas_call x1, Pallas kernels, on_device(): pl.pallas_call(kernel, out_shape=jax.ShapeDtypeStruct((2, 64, WIDTH), F32...  68.9 us
    squeeze x1, local copies, waits for them, and re-layouts, on_device(): result += [out[1, rows], out[0, rows]]  1.57 us

profile of v1, /device:TPU:1, one launch (start us, length us, event | category | flops | bytes accessed | tf_op | source)
XLA Modules:
  0.0 71.2 jit_solution(11744296369173638893)
XLA Ops:
  0.6 68.9 %shard_map.206 = f32[2,64,512]{2,1,0:T(8,128)} custom-call(bf16[1024,512]{1,0:T(8,128)(2,1)} %bitcast.22, bf16[1024,512]{1,0:T(8,128)(2,1)} %bitcast.23, bf16[1024,512]{1,0:T(8,128)(2,1)} %bitcast.24, bf16[1024,512]{1,0:T(8,128)(2,1)} %bitcast.25, bf16[1024,512]{1,0:T(8,128)(2,1)} %bitcast.26, bf16[1024,512]{1,0:T(8,128)(2,1)} %bitcast.27, s32[4]{0:T(128)} %flags.1, ...), custom_call_target="tpu_custom_call" | custom-call | tf_op jit(solution)/shard_map/pallas_call | solution.py:445
  69.6 1.6 %slice_bitcast_fusion = (f32[16,512]{1,0:T(8,128)}, f32[16,512]{1,0:T(8,128)}, f32[16,512]{1,0:T(8,128)}, f32[16,512]{1,0:T(8,128)}, f32[16,512]{1,0:T(8,128)}, ...) fusion(f32[2,64,512]{2,1,0:T(8,128)} %shard_map.206), kind=kLoop, calls=%fused_computation | loop fusion | bytes 524288 | tf_op jit(solution)/shard_map/squeeze | solution.py:478

commit v2 on v1

--- a/solution.py
+++ b/solution.py
@@ -68,8 +68,9 @@
 
 def kernel(
     x_hbm, q_hbm, k_hbm, v_hbm, do_hbm, dc_hbm, flags,
-    down_q, up_q, down_k, up_k, down_v, up_v, down_o, up_o,
+    down_q_hbm, up_q_hbm, down_k_hbm, up_k_hbm, down_v_hbm, up_v_hbm, down_o_hbm, up_o_hbm,
     out_ref,
+    firsts, seconds,
     xb, qb, kb, vb, dob, dcb,
     kv_stage, kv_in,
     part, sib_in, acc, y_in, total,
@@ -78,8 +79,8 @@
     grads, back, back_in, up_sum,
     cut, x_in, x_sum, z_in, z_all, x_all,
     load_sem, kv_send, kv_recv, lp_send, lp_recv, back_send, back_recv,
-    sib_send, sib_recv, y1_send, y1_recv, y2_send, y2_recv, fw_send, fw_recv,
-    x1_send, x1_recv, z1_send, z1_recv, z2_send, z2_recv, x2_send, x2_recv,
+    sib_send, sib_recv, y_send, y_recv, fw_send, fw_recv,
+    x1_send, x1_recv, z_send, z_recv, x2_send, x2_recv,
 ):
     ctx, head, dp = lax.axis_index("ctx"), lax.axis_index("head"), lax.axis_index("dp")
     y, core = head // 2, head % 2
@@ -100,13 +101,22 @@
         return {"ctx": (other % 2) * NZ + z, "dp": other // 2}
 
     loads = []
-    pairs = [(x_hbm, xb), (do_hbm, dob)]
-    for source, target in ((k_hbm, kb), (v_hbm, vb), (q_hbm, qb), (dc_hbm, dcb)):
-        pairs += [(source.at[:, pl.ds(HD * h, HD)], target.at[h]) for h in range(4)]
-    for i, (source, target) in enumerate(pairs):
-        copy = pltpu.make_async_copy(source, target, load_sem.at[i])
-        copy.start()
-        loads.append(copy)
+
+    def load(*pairs):
+        for source, target in pairs:
+            copy = pltpu.make_async_copy(source, target, load_sem.at[len(loads)])
+            copy.start()
+            loads.append(copy)
+
+    def by_head(source, target):
+        return [(source.at[:, pl.ds(HD * h, HD)], target.at[h]) for h in range(4)]
+
+    load(
+        (down_q_hbm, firsts.at[0]), (down_k_hbm, firsts.at[1]), (down_v_hbm, firsts.at[2]), (up_o_hbm, firsts.at[3]),
+        (x_hbm, xb), (do_hbm, dob),
+        (up_q_hbm, seconds.at[0]), (up_k_hbm, seconds.at[1]), (up_v_hbm, seconds.at[2]), (down_o_hbm, seconds.at[3]),
+        *by_head(k_hbm, kb), *by_head(v_hbm, vb),
+    )
 
     barrier = pltpu.get_barrier_semaphore()
     peers = [sibling]
@@ -145,10 +155,101 @@
         f3 + (1 - f3) * 3,
     )
 
+    def own_latents(owner):
+        first = firsts[...].reshape(4 * RANK, WIDTH)
+        for j in range(2):
+            rows = pl.ds(pl.multiple_of(owner * 256 + HALF * j, 256), 256)
+            lat_part = dot(first[: 3 * RANK], xb[rows, :], NT)
+            mix_part = dot(first[3 * RANK :], dob[rows, :], NT)
+            for k in range(2):
+                part[0, owner * 4 + 2 * j + k, : 3 * RANK] = lat_part[:, HD * k : HD * (k + 1)]
+                part[0, owner * 4 + 2 * j + k, 3 * RANK :] = mix_part[:, HD * k : HD * (k + 1)]
+
+    for copy in loads[:6]:
+        copy.wait()
+    with jax.named_scope("own_latents"):
+        own_latents(1 - core)
+    with jax.named_scope("entry_barrier"):
+        pl.semaphore_wait(barrier, len(peers))
+
+    mine = core * 4
+    other = (1 - core) * 4
+
+    def sum_heads(p, late=None):
+        pair = (part.at[p, pl.ds(other, 4)], sib_in.at[p], sib_send.at[p], sib_recv.at[p], sibling)
+        send(*pair)
+        yield
+        remote(*pair).wait_recv()
+        extra = [0.0] * 4 if late is None else late()
+        for i in range(4):
+            acc[p, i] = (part[p, mine + i] + sib_in[p, i] + extra[i]).astype(BF16)
+        shares = [(acc.at[p], y_in.at[p, d - 1], y_send.at[p, d - 1], y_recv.at[p, d - 1], y_peer(d)) for d in range(1, NY)]
+        for share in shares:
+            send(*share)
+        yield
+        for share in shares:
+            remote(*share).wait_recv()
+        for i in range(4):
+            summed = acc[p, i].astype(F32)
+            for d in range(1, NY):
+                summed = summed + y_in[p, d - 1, i].astype(F32)
+            total[p, mine + i] = summed
+        own = total.at[p, pl.ds(mine, 4)]
+        send(own, own, fw_send.at[p], fw_recv.at[p], sibling)
+        yield
+        came = total.at[p, pl.ds(other, 4)]
+        remote(came, came, fw_send.at[p], fw_recv.at[p], sibling).wait_recv()
+        yield
+
+    def sum_tokens(e):
+        for d in range(1, NX):
+            send(cut.at[e, lax.rem(x + d, NX)], x_in.at[e, d - 1], x1_send.at[e, d - 1], x1_recv.at[e, d - 1], x_peer(d))
+        yield
+        summed = cut[e, x].astype(F32)
+        for d in range(1, NX):
+            remote(cut.at[e, 0], x_in.at[e, d - 1], x1_send.at[e, d - 1], x1_recv.at[e, d - 1], x_peer(d)).wait_recv()
+            summed = summed + x_in[e, d - 1].astype(F32)
+        x_sum[e] = summed.astype(BF16)
+        shares = [(x_sum.at[e], z_in.at[e, d - 1], z_send.at[e, d - 1], z_recv.at[e, d - 1], z_peer(d)) for d in range(1, NZ)]
+        for share in shares:
+            send(*share)
+        yield
+        summed = x_sum[e].astype(F32)
+        for d, share in enumerate(shares):
+            remote(*share).wait_recv()
+            summed = summed + z_in[e, d].astype(F32)
+        z_all[e] = summed.astype(BF16)
+        for d in range(1, NX):
+            send(z_all.at[e], x_all.at[e, x], x2_send.at[e, d - 1], x2_recv.at[e, d - 1], x_peer(d))
+        x_all[e, x] = z_all[e]
+        yield
+        for d in range(1, NX):
+            came = x_all.at[e, lax.rem(x + NX - d, NX)]
+            remote(z_all.at[e], came, x2_send.at[e, d - 1], x2_recv.at[e, d - 1], x_peer(d)).wait_recv()
+        for c in range(4):
+            out_ref[e, :, HD * c : HD * (c + 1)] = x_all[e, c].astype(F32)
+        yield
+
+    latents = sum_heads(0)
+    next(latents)
+    with jax.named_scope("own_latents"):
+        own_latents(core)
+
+    with jax.named_scope("stage_keys"):
+        for copy in loads[10:18]:
+            copy.wait()
+        for s in range(2):
+            for i, base in enumerate((kb, vb)):
+                kv_stage[s, i] = base[head_of[s], HALF:, :]
+            send(kv_stage.at[s], kv_in.at[s], kv_send.at[s], kv_recv.at[s], {"ctx": after})
+
+    load(*by_head(q_hbm, qb), *by_head(dc_hbm, dcb))
+    for copy in loads[6:10]:
+        copy.wait()
     up_pad[...] = jnp.zeros_like(up_pad)
-    for t, factor in enumerate((up_q, up_k, up_v, down_o)):
+    for t, factor in enumerate(seconds[t] for t in range(4)):
         for copy_at in (0, RANK):
-            up_pad[32 * t + copy_at : 32 * t + copy_at + RANK, WIDTH * t : WIDTH * (t + 1)] = factor[...]
+            up_pad[32 * t + copy_at : 32 * t + copy_at + RANK, WIDTH * t : WIDTH * (t + 1)] = factor
         for h in range(4):
             fac[t, h] = factor[:, HD * h : HD * (h + 1)]
     for t in range(2):
@@ -159,107 +260,14 @@
     back[...] = jnp.zeros_like(back)
     up_sum[...] = jnp.zeros_like(up_sum)
 
-    loads[0].wait()
-    first = jnp.concatenate([down_q[...], down_k[...], down_v[...]], axis=0)
-    lat_part = dot(first, xb[...], NT)
-    loads[1].wait()
-    mix_part = dot(up_o[...], dob[...], NT)
-    for b in range(8):
-        part[0, place(b), :48] = lat_part[:, HD * b : HD * (b + 1)]
-        part[0, place(b), 48:] = mix_part[:, HD * b : HD * (b + 1)]
-
-    pl.semaphore_wait(barrier, len(peers))
-
-    def sum_heads(p, late=None):
-        mine = core * 4
-        other = (1 - core) * 4
-        send(part.at[p, pl.ds(other, 4)], sib_in.at[p], sib_send.at[p], sib_recv.at[p], sibling)
-        yield
-        remote(part.at[p, pl.ds(other, 4)], sib_in.at[p], sib_send.at[p], sib_recv.at[p], sibling).wait_recv()
-        for i in range(4):
-            acc[p, i] = part[p, mine + i] + sib_in[p, i]
-        if late is not None:
-            late()
-        for d in range(1, NY):
-            send(acc.at[p, lax.rem(y + d, NY)], y_in.at[p, d - 1], y1_send.at[p, d - 1], y1_recv.at[p, d - 1], y_peer(d))
-        yield
-        for d in range(1, NY):
-            remote(acc.at[p, 0], y_in.at[p, d - 1], y1_send.at[p, d - 1], y1_recv.at[p, d - 1], y_peer(d)).wait_recv()
-        own = total.at[p, mine + y]
-        own[...] = acc[p, y] + y_in[p, 0] + y_in[p, 1] + y_in[p, 2]
-        for d in range(1, NY):
-            send(own, own, y2_send.at[p, d - 1], y2_recv.at[p, d - 1], y_peer(d))
-        send(own, own, fw_send.at[p, 0], fw_recv.at[p, 0], sibling)
-        yield
-        for d in range(1, NY):
-            came = total.at[p, mine + lax.rem(y + NY - d, NY)]
-            remote(came, came, y2_send.at[p, d - 1], y2_recv.at[p, d - 1], y_peer(d)).wait_recv()
-            send(came, came, fw_send.at[p, d], fw_recv.at[p, d], sibling)
-        yield
-        for d in range(NY):
-            came = total.at[p, other + lax.rem(y + NY - d, NY)]
-            remote(came, came, fw_send.at[p, d], fw_recv.at[p, d], sibling).wait_recv()
-        yield
-
-    def sum_tokens(e):
-        for d in range(1, NX):
-            send(cut.at[e, lax.rem(x + d, NX)], x_in.at[e, d - 1], x1_send.at[e, d - 1], x1_recv.at[e, d - 1], x_peer(d))
-        yield
-        for d in range(1, NX):
-            remote(cut.at[e, 0], x_in.at[e, d - 1], x1_send.at[e, d - 1], x1_recv.at[e, d - 1], x_peer(d)).wait_recv()
-        x_sum[e] = cut[e, x] + x_in[e, 0] + x_in[e, 1] + x_in[e, 2]
-        for d in range(1, NZ):
-            send(x_sum.at[e, lax.rem(z + d, NZ)], z_in.at[e, d - 1], z1_send.at[e, d - 1], z1_recv.at[e, d - 1], z_peer(d))
-        yield
-        for d in range(1, NZ):
-            remote(x_sum.at[e, 0], z_in.at[e, d - 1], z1_send.at[e, d - 1], z1_recv.at[e, d - 1], z_peer(d)).wait_recv()
-        own = z_all.at[e, z]
-        summed = x_sum[e, z]
-        for d in range(1, NZ):
-            summed = summed + z_in[e, d - 1]
-        own[...] = summed
-        for d in range(1, NZ):
-            send(own, own, z2_send.at[e, d - 1], z2_recv.at[e, d - 1], z_peer(d))
-        yield
-        for d in range(1, NZ):
-            came = z_all.at[e, lax.rem(z + NZ - d, NZ)]
-            remote(came, came, z2_send.at[e, d - 1], z2_recv.at[e, d - 1], z_peer(d)).wait_recv()
-        for d in range(1, NX):
-            send(z_all.at[e], x_all.at[e, x], x2_send.at[e, d - 1], x2_recv.at[e, d - 1], x_peer(d))
-        x_all[e, x] = z_all[e]
-        yield
-        for d in range(1, NX):
-            came = x_all.at[e, lax.rem(x + NX - d, NX)]
-            remote(z_all.at[e], came, x2_send.at[e, d - 1], x2_recv.at[e, d - 1], x_peer(d)).wait_recv()
-        for c in range(4):
-            for r in range(8):
-                out_ref[e, 8 * r : 8 * r + 8, HD * c : HD * (c + 1)] = x_all[e, c, r]
-        yield
-
-    latents = sum_heads(0)
-    next(latents)
-
-    for copy in loads[2:10]:
-        copy.wait()
-    for s in range(2):
-        for i, base in enumerate((kb, vb)):
-            kv_stage[s, i] = base[head_of[s], HALF:, :]
-        send(kv_stage.at[s], kv_in.at[s], kv_send.at[s], kv_recv.at[s], {"ctx": after})
-
-    for _ in range(4):
+    with jax.named_scope("latent_sum"):
         next(latents)
-
-    for c in range(2):
-        send(
-            total.at[0, pl.ds(4 * c + 2, 2), pl.ds(RANK, 2 * RANK)], lat_prev.at[pl.ds(2 * c, 2)],
-            lp_send.at[c], lp_recv.at[c], {"ctx": after},
-        )
-    for copy in loads[10:]:
-        copy.wait()
-
-    def adapt(b, carry):
+        next(latents)
+
+    def adapt(i, owner):
+        b = owner * 2 + i % 2 + 4 * (i // 2)
         rows = pl.ds(pl.multiple_of(b * HD, HD), HD)
-        both = split_rows(2.0 * total[0, place(b)], 4)
+        both = split_rows(2.0 * total[0, owner * 4 + i], 4)
         lat_low[:, rows] = both.astype(BF16)
         extra = dot(both.T.astype(BF16), up_pad[...])
         for t, (base, full, turned) in enumerate(
@@ -271,19 +279,30 @@
                 full[h, rows, :] = low
                 if turned is not None:
                     turned[h, :, rows] = low.T
-        return carry
-
-    lax.fori_loop(0, 8, adapt, 0)
-
+        return owner
+
+    for copy in loads[18:]:
+        copy.wait()
+    with jax.named_scope("adapt"):
+        lax.fori_loop(0, 4, adapt, core)
+    with jax.named_scope("latent_sum"):
+        next(latents)
     for c in range(2):
-        remote(
+        send(
             total.at[0, pl.ds(4 * c + 2, 2), pl.ds(RANK, 2 * RANK)], lat_prev.at[pl.ds(2 * c, 2)],
             lp_send.at[c], lp_recv.at[c], {"ctx": after},
-        ).wait_recv()
-    for b in range(4):
-        both = split_rows(2.0 * lat_prev[b], 2)
-        prev_low[:, HD * b : HD * (b + 1)] = both.astype(BF16)
-        prev_cols[HD * b : HD * (b + 1), :] = both.T.astype(BF16)
+        )
+    with jax.named_scope("adapt"):
+        lax.fori_loop(0, 4, adapt, 1 - core)
+        for c in range(2):
+            remote(
+                total.at[0, pl.ds(4 * c + 2, 2), pl.ds(RANK, 2 * RANK)], lat_prev.at[pl.ds(2 * c, 2)],
+                lp_send.at[c], lp_recv.at[c], {"ctx": after},
+            ).wait_recv()
+        for b in range(4):
+            both = split_rows(2.0 * lat_prev[b], 2)
+            prev_low[:, HD * b : HD * (b + 1)] = both.astype(BF16)
+            prev_cols[HD * b : HD * (b + 1), :] = both.T.astype(BF16)
 
     def attend(slot, h, first_at, off):
         last_at = HALF - first_at
@@ -370,63 +389,71 @@
     def both_kinds(i, carry):
         h = head_of[0] + i * (head_of[1] - head_of[0])
         still = head_of[2] + i * (head_of[3] - head_of[2])
-        remote(kv_stage.at[i], kv_in.at[i], kv_send.at[i], kv_recv.at[i], {"ctx": after}).wait_recv()
+        with jax.named_scope("wait_keys"):
+            remote(kv_stage.at[i], kv_in.at[i], kv_send.at[i], kv_recv.at[i], {"ctx": after}).wait_recv()
         off_k = (kv_in[i, 0].astype(F32) + dot(prev_cols[...], prev_up[0, h])).astype(BF16)
         off_v = (kv_in[i, 1].astype(F32) + dot(prev_cols[...], prev_up[1, h])).astype(BF16)
-        attend(i, h, HALF, (off_k, off_v, off_k.T, off_v.T))
+        with jax.named_scope("attend_shifted"):
+            attend(i, h, HALF, (off_k, off_v, off_k.T, off_v.T))
 
         @pl.when(i == 1)
         def _():
             for c in range(2):
                 back_copy(c).start()
 
-        attend(2 + i, still, 0, None)
+        with jax.named_scope("attend_still"):
+            attend(2 + i, still, 0, None)
         return carry
 
     lax.fori_loop(0, 2, both_kinds, 0)
 
-    for b in range(8):
-        part[1, place(b)] = grads[:, HD * b : HD * (b + 1)]
-
-    def add_back():
-        for c in range(2):
-            remote(back.at[c], back_in.at[c], back_send.at[c], back_recv.at[c], sibling).wait_recv()
-        for i in range(2):
-            acc[1, 2 + i, RANK : 3 * RANK] += back_in[0, i] + back_in[1, i]
-
-    shares = sum_heads(1, add_back)
-    next(shares)
-    for h in range(4):
-        piece = up_sum[jnp.minimum(slot_of[h], 3)]
-        for r in range(8):
-            cut[0, h, r] = piece[8 * r : 8 * r + 8]
-    ups = sum_tokens(0)
-    next(ups)
-    next(shares)
-    next(ups)
-    next(shares)
-    next(ups)
-    next(shares)
-    next(shares)
-
-    wide = []
-    for b in range(8):
-        wide.append(split_rows(2.0 * total[1, place(b)], 4).astype(BF16))
-    wide = jnp.concatenate(wide, axis=1)
-    down = dot(wide[:96], xb[...])
-    last = fold(dot(wide[96:], dob[...]))
-    down = jnp.concatenate([fold(down[32 * t : 32 * t + 32]) for t in range(3)] + [last], axis=0)
-    for c in range(4):
-        for r in range(8):
-            cut[1, c, r] = down[8 * r : 8 * r + 8, HD * c : HD * (c + 1)]
-    downs = sum_tokens(1)
-    next(downs)
-    next(ups)
-    next(downs)
-    next(downs)
-    next(ups)
-    next(downs)
-    next(downs)
+    with jax.named_scope("share_sum"):
+        for b in range(8):
+            part[1, place(b)] = grads[:, HD * b : HD * (b + 1)]
+
+        def add_back():
+            for c in range(2):
+                remote(back.at[c], back_in.at[c], back_send.at[c], back_recv.at[c], sibling).wait_recv()
+            none = jnp.zeros((RANK, HD), F32)
+            return [0.0, 0.0] + [
+                jnp.concatenate([none, back_in[0, i] + back_in[1, i], none], axis=0) for i in range(2)
+            ]
+
+        shares = sum_heads(1, add_back)
+        next(shares)
+        for h in range(4):
+            cut[0, h] = up_sum[jnp.minimum(slot_of[h], 3)].astype(BF16)
+        ups = sum_tokens(0)
+        next(ups)
+        next(shares)
+        next(ups)
+        next(shares)
+
+    def down_gradients(owner):
+        wide = jnp.concatenate([split_rows(2.0 * total[1, owner * 4 + i], 4).astype(BF16) for i in range(4)], axis=1)
+        down = jnp.zeros((96, WIDTH), F32)
+        last = jnp.zeros((32, WIDTH), F32)
+        for j in range(2):
+            rows = pl.ds(pl.multiple_of(owner * 256 + HALF * j, 256), 256)
+            here = wide[:, 256 * j : 256 * (j + 1)]
+            down = down + dot(here[:96], xb[rows, :])
+            last = last + dot(here[96:], dob[rows, :])
+        return jnp.concatenate([fold(down[32 * t : 32 * t + 32]) for t in range(3)] + [fold(last)], axis=0)
+
+    with jax.named_scope("down_gradients"):
+        down = down_gradients(core)
+        next(shares)
+        down = down + down_gradients(1 - core)
+        for c in range(4):
+            cut[1, c] = down[:, HD * c : HD * (c + 1)].astype(BF16)
+    with jax.named_scope("token_sum"):
+        downs = sum_tokens(1)
+        next(downs)
+        next(ups)
+        next(downs)
+        next(ups)
+        next(downs)
+        next(downs)
     for copy in sends:
         copy.wait_send()
     for c in range(2):
@@ -445,25 +472,26 @@
     out = pl.pallas_call(
         kernel,
         out_shape=jax.ShapeDtypeStruct((2, 64, WIDTH), F32),
-        in_specs=[anywhere] * 6 + [smem] + [vmem] * 8,
+        in_specs=[anywhere] * 6 + [smem] + [anywhere] * 8,
         out_specs=vmem,
         scratch_shapes=[
-            *[v((ROWS, WIDTH), BF16) for _ in range(1)], *[v((4, ROWS, HD), BF16) for _ in range(3)],
+            v((4, RANK, WIDTH), BF16), v((4, RANK, WIDTH), BF16),
+            v((ROWS, WIDTH), BF16), *[v((4, ROWS, HD), BF16) for _ in range(3)],
             v((ROWS, WIDTH), BF16), v((4, ROWS, HD), BF16),
             v((2, 2, HALF, HD), BF16), v((2, 2, HALF, HD), BF16),
-            v((2, 8, 64, HD), F32), v((2, 4, 64, HD), F32), v((2, 4, 64, HD), F32),
-            v((2, 3, 64, HD), F32), v((2, 8, 64, HD), F32),
+            v((2, 8, 64, HD), F32), v((2, 4, 64, HD), F32), v((2, 4, 64, HD), BF16),
+            v((2, 3, 4, 64, HD), BF16), v((2, 8, 64, HD), F32),
             v((4, 32, HD), F32), v((128, 4 * WIDTH), BF16), v((4, 4, RANK, HD), BF16),
             v((2, 4, 64, HD), BF16), v((128, ROWS), BF16),
             v((64, HALF), BF16), v((HALF, 64), BF16),
             *[v((4, ROWS, HD), BF16) for _ in range(4)],
             *[v((4, HD, ROWS), BF16) for _ in range(2)],
             v((64, ROWS), F32), v((2, 2, 32, HD), F32), v((2, 2, 32, HD), F32), v((4, 64, HD), F32),
-            v((2, 4, 8, 8, HD), F32), v((2, 3, 8, 8, HD), F32), v((2, 8, 8, HD), F32),
-            v((2, 7, 8, HD), F32), v((2, 8, 8, HD), F32), v((2, 4, 8, 8, HD), F32),
-            dma((18,)), dma((2,)), dma((2,)), dma((2,)), dma((2,)), dma((2,)), dma((2,)),
-            dma((2,)), dma((2,)), dma((2, 3)), dma((2, 3)), dma((2, 3)), dma((2, 3)), dma((2, 4)), dma((2, 4)),
-            dma((2, 3)), dma((2, 3)), dma((2, 7)), dma((2, 7)), dma((2, 7)), dma((2, 7)), dma((2, 3)), dma((2, 3)),
+            v((2, 4, 64, HD), BF16), v((2, 3, 64, HD), BF16), v((2, 64, HD), BF16),
+            v((2, 7, 64, HD), BF16), v((2, 64, HD), BF16), v((2, 4, 64, HD), BF16),
+            dma((26,)), dma((2,)), dma((2,)), dma((2,)), dma((2,)), dma((2,)), dma((2,)),
+            dma((2,)), dma((2,)), dma((2, 3)), dma((2, 3)), dma((2,)), dma((2,)),
+            dma((2, 3)), dma((2, 3)), dma((2, 7)), dma((2, 7)), dma((2, 3)), dma((2, 3)),
         ],
         compiler_params=pltpu.CompilerParams(
             collective_id=0, has_side_effects=True, vmem_limit_bytes=56 * 1024 * 1024

time: 72.4 us -> 65 us (0.90)
  Pallas kernels: 68.9 us -> 61.8 us
    pallas_call x1, Pallas kernels: 68.9 us -> 61.8 us  [on_device(): pl.pallas_call(kernel, out_shape=jax.ShapeDtypeStruct((2, 64, WIDTH), F32...]
where the time goes in v2:
time: 65 us; the launch traced here: 64 us
  Pallas kernels  61.8 us (95%)
  local copies, waits for them, and re-layouts  1.57 us (2%)
  between operations  0.65 us (1%)
    pallas_call x1, Pallas kernels, on_device(): pl.pallas_call(kernel, out_shape=jax.ShapeDtypeStruct((2, 64, WIDTH), F32...  61.8 us
    squeeze x1, local copies, waits for them, and re-layouts, on_device(): result += [out[1, rows], out[0, rows]]  1.57 us

profile of v2, /device:TPU:1, one launch (start us, length us, event | category | flops | bytes accessed | tf_op | source)
XLA Modules:
  0.0 64.0 jit_solution(16090389457958599235)
XLA Ops:
  0.6 61.8 %shard_map.206 = f32[2,64,512]{2,1,0:T(8,128)} custom-call(bf16[1024,512]{1,0:T(8,128)(2,1)} %bitcast.22, bf16[1024,512]{1,0:T(8,128)(2,1)} %bitcast.23, bf16[1024,512]{1,0:T(8,128)(2,1)} %bitcast.24, bf16[1024,512]{1,0:T(8,128)(2,1)} %bitcast.25, bf16[1024,512]{1,0:T(8,128)(2,1)} %bitcast.26, bf16[1024,512]{1,0:T(8,128)(2,1)} %bitcast.27, s32[4]{0:T(128)} %flags.1, ...), custom_call_target="tpu_custom_call" | custom-call | tf_op jit(solution)/shard_map/pallas_call | solution.py:472
  62.4 1.6 %slice_bitcast_fusion = (f32[16,512]{1,0:T(8,128)}, f32[16,512]{1,0:T(8,128)}, f32[16,512]{1,0:T(8,128)}, f32[16,512]{1,0:T(8,128)}, f32[16,512]{1,0:T(8,128)}, ...) fusion(f32[2,64,512]{2,1,0:T(8,128)} %shard_map.206), kind=kLoop, calls=%fused_computation | loop fusion | bytes 524288 | tf_op jit(solution)/shard_map/squeeze | solution.py:506

commit v3 on v2

--- a/solution.py
+++ b/solution.py
@@ -12,6 +12,7 @@
 ROWS = 1024
 HALF = 512
 CHUNK = 256
+STRIP = 64
 RANK = 16
 WIDTH = 512
 NY, NZ, NX = 4, 8, 4
@@ -45,25 +46,17 @@
     return pair[:RANK] + pair[RANK:]
 
 
-def chunk_scores(keys, values, keys_t, values_t, query, upstream):
-    length = keys.shape[0]
-    scores = dot(keys, query, NT)
-    own = scores[length - CHUNK :]
-    causal = lax.broadcasted_iota(jnp.int32, own.shape, 0) <= lax.broadcasted_iota(
-        jnp.int32, own.shape, 1
-    )
-    own = jnp.where(causal, own, -jnp.inf)
-    scores = own if length == CHUNK else jnp.concatenate([scores[: length - CHUNK], own], axis=0)
-    peak = jnp.max(scores, axis=0, keepdims=True)
-    weights = jnp.exp2((scores - peak) * EXP_SCALE)
-    probs = weights * (1.0 / jnp.sum(weights, axis=0, keepdims=True))
-    grad_probs = dot(values, upstream, NT)
-    center = jnp.sum(probs * grad_probs, axis=0, keepdims=True)
-    grad_scores = (probs * (grad_probs - center) * SCALE).astype(BF16)
-    probs_low = probs.astype(BF16)
-    context_t = dot(values_t, probs_low)
-    grad_query_t = dot(keys_t, grad_scores)
-    return probs_low, grad_scores, context_t.astype(BF16), grad_query_t.astype(BF16)
+def fold_strip(strip, op):
+    strip = strip.reshape(STRIP // 8, 8, CHUNK)
+    result = strip[0]
+    for i in range(1, STRIP // 8):
+        result = op(result, strip[i])
+    return result
+
+
+def merged(*lists):
+    timed = [((i + 0.5) / len(steps), k, step) for k, steps in enumerate(lists) for i, step in enumerate(steps)]
+    return [step for _, _, step in sorted(timed, key=lambda item: item[:2])]
 
 
 def kernel(
@@ -76,7 +69,9 @@
     part, sib_in, acc, y_in, total,
     lat_prev, up_pad, fac, prev_up, lat_low, prev_low, prev_cols,
     qa, ka, va, ua, kt, vt,
-    grads, back, back_in, up_sum,
+    grad_q, grad_k, grad_v, ctx_all, back_k, back_v, off_rows, off_cols,
+    score, grad_prob, prob_low, grad_low,
+    back, back_in, up_sum,
     cut, x_in, x_sum, z_in, z_all, x_all,
     load_sem, kv_send, kv_recv, lp_send, lp_recv, back_send, back_recv,
     sib_send, sib_recv, y_send, y_recv, fw_send, fw_recv,
@@ -234,6 +229,8 @@
     next(latents)
     with jax.named_scope("own_latents"):
         own_latents(core)
+    with jax.named_scope("latent_sum"):
+        next(latents)
 
     with jax.named_scope("stage_keys"):
         for copy in loads[10:18]:
@@ -256,12 +253,8 @@
         for h in range(4):
             at = WIDTH * (1 + t) + HD * h
             prev_up[t, h] = up_pad[32:96, at : at + HD]
-    grads[...] = jnp.zeros_like(grads)
-    back[...] = jnp.zeros_like(back)
-    up_sum[...] = jnp.zeros_like(up_sum)
 
     with jax.named_scope("latent_sum"):
-        next(latents)
         next(latents)
 
     def adapt(i, owner):
@@ -304,81 +297,117 @@
             prev_low[:, HD * b : HD * (b + 1)] = both.astype(BF16)
             prev_cols[HD * b : HD * (b + 1), :] = both.T.astype(BF16)
 
-    def attend(slot, h, first_at, off):
-        last_at = HALF - first_at
-        uq, uk, uv, od = (fac[t, h] for t in range(4))
-        off_k, off_v, off_kt, off_vt = off if off is not None else (
-            ka[h, :HALF, :], va[h, :HALF, :], kt[h, :, :HALF], vt[h, :, :HALF],
-        )
-        sums = [0.0, 0.0, 0.0, 0.0]
-
-        def keys_done(t, factor, grad, lat, put):
-            low = grad.astype(BF16)
-            put(t, dot(factor, low, NT))
-            sums[t] = sums[t] + fold(dot(lat, low))
-
-        def queries_done(t, factor, grad_t, lat, put):
-            put(t, dot(factor, grad_t))
-            sums[t] = sums[t] + fold(dot(lat, grad_t, NT))
-
-        def lat_of(t, at):
-            return lat_low[32 * t : 32 * t + 32, at : at + HALF]
-
-        def put_at(at):
-            def put(t, value):
-                grads[RANK * t : RANK * (t + 1), at : at + HALF] += value
-            return put
-
-        def put_back(t, value):
-            for b in range(4):
-                back[b // 2, b % 2, RANK * (t - 1) : RANK * t] += value[:, HD * b : HD * (b + 1)]
-
-        for at, with_off in ((first_at, False), (last_at, True)):
-            own = slice(at, at + HALF)
-            keys, values = ka[h, own, :], va[h, own, :]
-            keys_t, values_t = kt[h, :, own], vt[h, :, own]
-            query, upstream = qa[h, own, :], ua[h, own, :]
-            ahead = 0
-            if with_off:
-                ahead = HALF
-                keys = jnp.concatenate([off_k, keys], axis=0)
-                values = jnp.concatenate([off_v, values], axis=0)
-                keys_t = jnp.concatenate([off_kt, keys_t], axis=1)
-                values_t = jnp.concatenate([off_vt, values_t], axis=1)
-            results = []
-            for c in range(2):
-                length = ahead + CHUNK * (c + 1)
-                here = slice(CHUNK * c, CHUNK * (c + 1))
-                results.append(
-                    chunk_scores(
-                        keys[:length], values[:length], keys_t[:, :length], values_t[:, :length],
-                        query[here], upstream[here],
-                    )
-                )
-            short = ahead + CHUNK
-            (p0, s0, c0, q0), (p1, s1, c1, q1) = results
-
-            def over_queries(early, late, rows):
-                return jnp.concatenate(
-                    [
-                        dot(early, rows[:CHUNK]) + dot(late[:short], rows[CHUNK:]),
-                        dot(late[short:], rows[CHUNK:]),
-                    ],
-                    axis=0,
-                )
-
-            grad_keys = over_queries(s0, s1, query)
-            grad_values = over_queries(p0, p1, upstream)
-            queries_done(0, uq, jnp.concatenate([q0, q1], axis=1), lat_of(0, at), put_at(at))
-            queries_done(3, od, jnp.concatenate([c0, c1], axis=1), lat_of(3, at), put_at(at))
-            for t, factor, grad in ((1, uk, grad_keys), (2, uv, grad_values)):
-                keys_done(t, factor, grad[ahead:], lat_of(t, at), put_at(at))
-                if with_off and off is None:
-                    keys_done(t, factor, grad[:ahead], lat_of(t, 0), put_at(0))
-                elif with_off:
-                    keys_done(t, factor, grad[:ahead], prev_low[32 * t - 32 : 32 * t, :], put_back)
-        for t in range(4):
-            up_sum[slot, RANK * t : RANK * (t + 1)] = sums[t]
+    def chunk(j, slot, at, with_off, c, sums):
+        h = head_of[slot]
+        off = slot if slot < 2 else None
+        s, g, p, ds = (ref.at[j % 2] for ref in (score, grad_prob, prob_low, grad_low))
+        ahead = HALF if with_off else 0
+        length = ahead + CHUNK * (c + 1)
+        strips = length // STRIP
+        here = slice(at + CHUNK * c, at + CHUNK * (c + 1))
+        held = {}
+
+        def key_rows(t, b):
+            first = CHUNK * b
+            if first >= ahead:
+                return (ka, va)[t][h, at + first - ahead : at + first - ahead + CHUNK, :]
+            if off is not None:
+                return off_rows[off, t, first : first + CHUNK]
+            return (ka, va)[t][h, first : first + CHUNK, :]
+
+        def key_cols(t):
+            own = (kt, vt)[t][h, :, at : at + length - ahead]
+            if not with_off:
+                return own
+            early = off_cols[off, t] if off is not None else (kt, vt)[t][h, :, :HALF]
+            return jnp.concatenate([early, own], axis=1)
+
+        def strip(i):
+            return slice(STRIP * i, STRIP * (i + 1))
+
+        def scores_of(b):
+            s[CHUNK * b : CHUNK * (b + 1), :] = dot(key_rows(0, b), qa[h, here, :], NT)
+
+        def grad_probs_of(b):
+            g[CHUNK * b : CHUNK * (b + 1), :] = dot(key_rows(1, b), ua[h, here, :], NT)
+
+        def causal(i):
+            value = s[strip(i), :]
+            first = STRIP * i - (length - CHUNK)
+            if first < 0:
+                return value
+            key = lax.broadcasted_iota(jnp.int32, value.shape, 0) + first
+            return jnp.where(key <= lax.broadcasted_iota(jnp.int32, value.shape, 1), value, -jnp.inf)
+
+        def peaks(i):
+            peak = fold_strip(causal(i), jnp.maximum)
+            held["peak"] = peak if i == 0 else jnp.maximum(held["peak"], peak)
+
+        def weigh(i):
+            if i == 0:
+                held["peak"] = jnp.max(held["peak"], axis=0, keepdims=True)
+                held["sum"] = held["center"] = jnp.zeros((8, CHUNK), F32)
+            weights = jnp.exp2((causal(i) - held["peak"]) * EXP_SCALE)
+            s[strip(i), :] = weights
+            held["sum"] = held["sum"] + fold_strip(weights, jnp.add)
+            held["center"] = held["center"] + fold_strip(weights * g[strip(i), :], jnp.add)
+
+        def finish(i):
+            if i == 0:
+                held["inverse"] = 1.0 / jnp.sum(held["sum"], axis=0, keepdims=True)
+                held["center"] = jnp.sum(held["center"], axis=0, keepdims=True) * held["inverse"]
+                held["scaled"] = held["inverse"] * SCALE
+            weights = s[strip(i), :]
+            p[strip(i), :] = (weights * held["inverse"]).astype(BF16)
+            ds[strip(i), :] = ((weights * held["scaled"]) * (g[strip(i), :] - held["center"])).astype(BF16)
+
+        def query_side():
+            grad_q[slot, :, here] = dot(key_cols(0), ds[:length, :]).astype(BF16)
+
+        def context_side():
+            ctx_all[slot, :, here] = dot(key_cols(1), p[:length, :]).astype(BF16)
+
+        def key_side(t, b):
+            low, rows = ((ds, qa), (p, ua))[t]
+            value = dot(low[CHUNK * b : CHUNK * (b + 1), :], rows[h, here, :])
+            name = (t, with_off, b)
+            sums[name] = sums[name] + value if name in sums else value
+
+        blocks = range(length // CHUNK)
+        before_it = [functools.partial(f, b) for b in blocks for f in (scores_of, grad_probs_of)]
+        middle = [functools.partial(f, i) for f in (peaks, weigh, finish) for i in range(strips)]
+        after_it = [query_side, context_side] + [functools.partial(key_side, t, b) for b in blocks for t in (0, 1)]
+        return before_it, middle, after_it
+
+    def keys_done(slot, sums):
+        for t, (grad, away) in enumerate(((grad_k, back_k), (grad_v, back_v))):
+            for b in range(2):
+                early, late = slice(CHUNK * b, CHUNK * (b + 1)), slice(HALF + CHUNK * b, HALF + CHUNK * (b + 1))
+                first, off, last = sums[t, False, b], sums[t, True, b], sums[t, True, b + 2]
+                if slot < 2:
+                    away[slot, early] = off.astype(BF16)
+                    grad[slot, early] = last.astype(BF16)
+                    grad[slot, late] = first.astype(BF16)
+                else:
+                    grad[slot, early] = (first + off).astype(BF16)
+                    grad[slot, late] = last.astype(BF16)
+
+    def factors(t, slots):
+        return jnp.concatenate([fac[t, head_of[slot]] for slot in slots], axis=1)
+
+    def stacked(ref, slots):
+        return jnp.concatenate([ref[slot] for slot in slots], axis=0)
+
+    def beside(ref, slots):
+        return jnp.concatenate([ref[slot] for slot in slots], axis=1)
+
+    def projections(slots):
+        return [
+            dot(factors(0, slots), stacked(grad_q, slots)),
+            dot(factors(1, slots), beside(grad_k, slots), NT),
+            dot(factors(2, slots), beside(grad_v, slots), NT),
+            dot(factors(3, slots), stacked(ctx_all, slots)),
+        ]
 
     def back_copy(c):
         return remote(
@@ -386,30 +415,59 @@
             {"ctx": before, "head": y * 2 + c},
         )
 
-    def both_kinds(i, carry):
-        h = head_of[0] + i * (head_of[1] - head_of[0])
-        still = head_of[2] + i * (head_of[3] - head_of[2])
-        with jax.named_scope("wait_keys"):
-            remote(kv_stage.at[i], kv_in.at[i], kv_send.at[i], kv_recv.at[i], {"ctx": after}).wait_recv()
-        off_k = (kv_in[i, 0].astype(F32) + dot(prev_cols[...], prev_up[0, h])).astype(BF16)
-        off_v = (kv_in[i, 1].astype(F32) + dot(prev_cols[...], prev_up[1, h])).astype(BF16)
-        with jax.named_scope("attend_shifted"):
-            attend(i, h, HALF, (off_k, off_v, off_k.T, off_v.T))
-
-        @pl.when(i == 1)
-        def _():
+    def keys_from_before(slot):
+        remote(
+            kv_stage.at[slot], kv_in.at[slot], kv_send.at[slot], kv_recv.at[slot], {"ctx": after}
+        ).wait_recv()
+        for t in range(2):
+            extra = dot(prev_cols[...], prev_up[t, head_of[slot]])
+            low = (kv_in[slot, t].astype(F32) + extra).astype(BF16)
+            off_rows[slot, t] = low
+            off_cols[slot, t] = low.T
+
+    def send_back():
+        for t, ref in ((1, back_k), (2, back_v)):
+            value = dot(factors(t, (0, 1)), beside(ref, (0, 1)), NT)
+            for b in range(4):
+                back[b // 2, b % 2, RANK * (t - 1) : RANK * t] = value[:, HD * b : HD * (b + 1)]
+        for c in range(2):
+            back_copy(c).start()
+
+    with jax.named_scope("attend"):
+        chunks, at_start, at_end, shares = [], {}, {}, []
+        all_sums = [{}, {}, {}, {}]
+        order = [(0, False), (1, False), (0, True), (1, True), (2, False), (2, True), (3, False), (3, True)]
+        for slot, with_off in order:
+            first_at = HALF if slot < 2 else 0
+            if slot < 2 and with_off:
+                at_start[len(chunks)] = functools.partial(keys_from_before, slot)
             for c in range(2):
-                back_copy(c).start()
-
-        with jax.named_scope("attend_still"):
-            attend(2 + i, still, 0, None)
-        return carry
-
-    lax.fori_loop(0, 2, both_kinds, 0)
+                at = HALF - first_at if with_off else first_at
+                chunks.append(chunk(len(chunks), slot, at, with_off, c, all_sums[slot]))
+            if with_off:
+                at_end[len(chunks) - 1] = functools.partial(keys_done, slot, all_sums[slot])
+        count = len(chunks)
+        for step in chunks[0][0]:
+            step()
+        for j in range(count + 1):
+            if j + 1 in at_start:
+                at_start[j + 1]()
+            lists = [chunks[j][1]] if j < count else []
+            lists += [chunks[j + 1][0]] if j + 1 < count else []
+            lists += [chunks[j - 1][2]] if j else []
+            for step in merged(*lists):
+                step()
+            if j - 1 in at_end:
+                at_end[j - 1]()
+            if j - 1 == 7:
+                send_back()
+            if j == count - 1:
+                shares = projections((0, 1))
+        wide = jnp.concatenate([a + b for a, b in zip(shares, projections((2, 3)))], axis=0)
 
     with jax.named_scope("share_sum"):
         for b in range(8):
-            part[1, place(b)] = grads[:, HD * b : HD * (b + 1)]
+            part[1, place(b)] = wide[:, HD * b : HD * (b + 1)]
 
         def add_back():
             for c in range(2):
@@ -421,13 +479,26 @@
 
         shares = sum_heads(1, add_back)
         next(shares)
+        next(shares)
+        every = (0, 1, 2, 3)
+        up_rows = [
+            fold(dot(lat_low[:32, :], stacked(grad_q, every), NT)),
+            fold(dot(lat_low[32:64, :], beside(grad_k, every))),
+            fold(dot(lat_low[64:96, :], beside(grad_v, every))),
+            fold(dot(lat_low[96:, :], stacked(ctx_all, every), NT)),
+        ]
+        for t, ref in ((1, back_k), (2, back_v)):
+            extra = fold(dot(prev_low[32 * t - 32 : 32 * t, :], beside(ref, (0, 1))))
+            up_rows[t] = up_rows[t] + jnp.concatenate([extra, jnp.zeros_like(extra)], axis=1)
+        up_rows = jnp.concatenate(up_rows, axis=0)
+        for slot in every:
+            up_sum[slot] = up_rows[:, HD * slot : HD * (slot + 1)]
         for h in range(4):
             cut[0, h] = up_sum[jnp.minimum(slot_of[h], 3)].astype(BF16)
         ups = sum_tokens(0)
         next(ups)
         next(shares)
         next(ups)
-        next(shares)
 
     def down_gradients(owner):
         wide = jnp.concatenate([split_rows(2.0 * total[1, owner * 4 + i], 4).astype(BF16) for i in range(4)], axis=1)
@@ -486,7 +557,10 @@
             v((64, HALF), BF16), v((HALF, 64), BF16),
             *[v((4, ROWS, HD), BF16) for _ in range(4)],
             *[v((4, HD, ROWS), BF16) for _ in range(2)],
-            v((64, ROWS), F32), v((2, 2, 32, HD), F32), v((2, 2, 32, HD), F32), v((4, 64, HD), F32),
+            v((4, HD, ROWS), BF16), v((4, ROWS, HD), BF16), v((4, ROWS, HD), BF16), v((4, HD, ROWS), BF16),
+            v((2, HALF, HD), BF16), v((2, HALF, HD), BF16), v((2, 2, HALF, HD), BF16), v((2, 2, HD, HALF), BF16),
+            v((2, ROWS, CHUNK), F32), v((2, ROWS, CHUNK), F32), v((2, ROWS, CHUNK), BF16), v((2, ROWS, CHUNK), BF16),
+            v((2, 2, 32, HD), F32), v((2, 2, 32, HD), F32), v((4, 64, HD), F32),
             v((2, 4, 64, HD), BF16), v((2, 3, 64, HD), BF16), v((2, 64, HD), BF16),
             v((2, 7, 64, HD), BF16), v((2, 64, HD), BF16), v((2, 4, 64, HD), BF16),
             dma((26,)), dma((2,)), dma((2,)), dma((2,)), dma((2,)), dma((2,)), dma((2,)),

time: 65 us -> 64.1 us (0.986); the launches traced: 64 us -> 63.9 us
  no operation moved by 1% of the time
where the time goes in v3:
time: 64.1 us; the launch traced here: 63.9 us
  Pallas kernels  61.7 us (96%)
  local copies, waits for them, and re-layouts  1.57 us (2%)
  between operations  0.65 us (1%)
    pallas_call x1, Pallas kernels, on_device(): pl.pallas_call(kernel, out_shape=jax.ShapeDtypeStruct((2, 64, WIDTH), F32...  61.7 us
    squeeze x1, local copies, waits for them, and re-layouts, on_device(): result += [out[1, rows], out[0, rows]]  1.57 us

profile of v3, /device:TPU:1, one launch (start us, length us, event | category | flops | bytes accessed | tf_op | source)
XLA Modules:
  0.0 63.9 jit_solution(475925988302963610)
XLA Ops:
  0.6 61.7 %shard_map.206 = f32[2,64,512]{2,1,0:T(8,128)} custom-call(bf16[1024,512]{1,0:T(8,128)(2,1)} %bitcast.22, bf16[1024,512]{1,0:T(8,128)(2,1)} %bitcast.23, bf16[1024,512]{1,0:T(8,128)(2,1)} %bitcast.24, bf16[1024,512]{1,0:T(8,128)(2,1)} %bitcast.25, bf16[1024,512]{1,0:T(8,128)(2,1)} %bitcast.26, bf16[1024,512]{1,0:T(8,128)(2,1)} %bitcast.27, s32[4]{0:T(128)} %flags.1, ...), custom_call_target="tpu_custom_call" | custom-call | tf_op jit(solution)/shard_map/pallas_call | solution.py:543
  62.3 1.6 %slice_bitcast_fusion = (f32[16,512]{1,0:T(8,128)}, f32[16,512]{1,0:T(8,128)}, f32[16,512]{1,0:T(8,128)}, f32[16,512]{1,0:T(8,128)}, f32[16,512]{1,0:T(8,128)}, ...) fusion(f32[2,64,512]{2,1,0:T(8,128)} %shard_map.206), kind=kLoop, calls=%fused_computation | loop fusion | bytes 524288 | tf_op jit(solution)/shard_map/squeeze | solution.py:580

commit v4 on v3

--- a/solution.py
+++ b/solution.py
@@ -16,6 +16,8 @@
 RANK = 16
 WIDTH = 512
 NY, NZ, NX = 4, 8, 4
+Y_ORDER = X_ORDER = (2, 1, 3)
+Z_ORDER = (4, 3, 5, 2, 6, 1, 7)
 SCALE = 1.0 / math.sqrt(HD)
 EXP_SCALE = SCALE * math.log2(math.e)
 MESH = pl.DeviceIdType.MESH
@@ -60,10 +62,10 @@
 
 
 def kernel(
-    x_hbm, q_hbm, k_hbm, v_hbm, do_hbm, dc_hbm, flags,
+    x_hbm, q_hbm, k_hbm, v_hbm, do_hbm, dc_hbm, flags_hbm,
     down_q_hbm, up_q_hbm, down_k_hbm, up_k_hbm, down_v_hbm, up_v_hbm, down_o_hbm, up_o_hbm,
     out_ref,
-    firsts, seconds,
+    flags, firsts, seconds,
     xb, qb, kb, vb, dob, dcb,
     kv_stage, kv_in,
     part, sib_in, acc, y_in, total,
@@ -106,11 +108,16 @@
     def by_head(source, target):
         return [(source.at[:, pl.ds(HD * h, HD)], target.at[h]) for h in range(4)]
 
+    def rows_of(owner, j):
+        return pl.ds(pl.multiple_of(owner * 256 + HALF * j, 256), 256)
+
+    def by_owner(owner):
+        rows = [rows_of(owner, j) for j in range(2)]
+        return [(source.at[r], target.at[r]) for source, target in ((x_hbm, xb), (do_hbm, dob)) for r in rows]
+
     load(
         (down_q_hbm, firsts.at[0]), (down_k_hbm, firsts.at[1]), (down_v_hbm, firsts.at[2]), (up_o_hbm, firsts.at[3]),
-        (x_hbm, xb), (do_hbm, dob),
-        (up_q_hbm, seconds.at[0]), (up_k_hbm, seconds.at[1]), (up_v_hbm, seconds.at[2]), (down_o_hbm, seconds.at[3]),
-        *by_head(k_hbm, kb), *by_head(v_hbm, vb),
+        *by_owner(1 - core), *by_owner(core), (flags_hbm, flags),
     )
 
     barrier = pltpu.get_barrier_semaphore()
@@ -135,6 +142,95 @@
         copy = remote(*args)
         copy.start()
         sends.append(copy)
+
+    def own_latents(owner):
+        first = firsts[...].reshape(4 * RANK, WIDTH)
+        for j in range(2):
+            rows = rows_of(owner, j)
+            lat_part = dot(first[: 3 * RANK], xb[rows, :], NT)
+            mix_part = dot(first[3 * RANK :], dob[rows, :], NT)
+            for k in range(2):
+                part[0, owner * 4 + 2 * j + k, : 3 * RANK] = lat_part[:, HD * k : HD * (k + 1)]
+                part[0, owner * 4 + 2 * j + k, 3 * RANK :] = mix_part[:, HD * k : HD * (k + 1)]
+
+    for copy in loads[:8]:
+        copy.wait()
+    with jax.named_scope("own_latents"):
+        own_latents(1 - core)
+    with jax.named_scope("entry_barrier"):
+        pl.semaphore_wait(barrier, len(peers))
+
+    mine = core * 4
+    other = (1 - core) * 4
+
+    def sum_heads(p, late=None):
+        pair = (part.at[p, pl.ds(other, 4)], sib_in.at[p], sib_send.at[p], sib_recv.at[p], sibling)
+        send(*pair)
+        yield
+        remote(*pair).wait_recv()
+        extra = [0.0] * 4 if late is None else late()
+        for i in range(4):
+            acc[p, i] = (part[p, mine + i] + sib_in[p, i] + extra[i]).astype(BF16)
+        shares = [(acc.at[p], y_in.at[p, d - 1], y_send.at[p, d - 1], y_recv.at[p, d - 1], y_peer(d)) for d in Y_ORDER]
+        for share in shares:
+            send(*share)
+        yield
+        for share in shares:
+            remote(*share).wait_recv()
+        for i in range(4):
+            summed = acc[p, i].astype(F32)
+            for d in range(1, NY):
+                summed = summed + y_in[p, d - 1, i].astype(F32)
+            total[p, mine + i] = summed
+        own = total.at[p, pl.ds(mine, 4)]
+        send(own, own, fw_send.at[p], fw_recv.at[p], sibling)
+        yield
+        came = total.at[p, pl.ds(other, 4)]
+        remote(came, came, fw_send.at[p], fw_recv.at[p], sibling).wait_recv()
+        yield
+
+    def sum_tokens(e):
+        for d in X_ORDER:
+            send(cut.at[e, lax.rem(x + d, NX)], x_in.at[e, d - 1], x1_send.at[e, d - 1], x1_recv.at[e, d - 1], x_peer(d))
+        yield
+        summed = cut[e, x].astype(F32)
+        for d in range(1, NX):
+            remote(cut.at[e, 0], x_in.at[e, d - 1], x1_send.at[e, d - 1], x1_recv.at[e, d - 1], x_peer(d)).wait_recv()
+            summed = summed + x_in[e, d - 1].astype(F32)
+        x_sum[e] = summed.astype(BF16)
+        shares = [(x_sum.at[e], z_in.at[e, d - 1], z_send.at[e, d - 1], z_recv.at[e, d - 1], z_peer(d)) for d in Z_ORDER]
+        for share in shares:
+            send(*share)
+        yield
+        summed = x_sum[e].astype(F32)
+        for share in shares:
+            remote(*share).wait_recv()
+        for d in range(1, NZ):
+            summed = summed + z_in[e, d - 1].astype(F32)
+        z_all[e] = summed.astype(BF16)
+        for d in X_ORDER:
+            send(z_all.at[e], x_all.at[e, x], x2_send.at[e, d - 1], x2_recv.at[e, d - 1], x_peer(d))
+        x_all[e, x] = z_all[e]
+        yield
+        for d in range(1, NX):
+            came = x_all.at[e, lax.rem(x + NX - d, NX)]
+            remote(z_all.at[e], came, x2_send.at[e, d - 1], x2_recv.at[e, d - 1], x_peer(d)).wait_recv()
+        for c in range(4):
+            out_ref[e, :, HD * c : HD * (c + 1)] = x_all[e, c].astype(F32)
+        yield
+
+    latents = sum_heads(0)
+    next(latents)
+    load(
+        *by_head(k_hbm, kb), *by_head(v_hbm, vb),
+        (up_q_hbm, seconds.at[0]), (up_k_hbm, seconds.at[1]), (up_v_hbm, seconds.at[2]), (down_o_hbm, seconds.at[3]),
+    )
+    for copy in loads[8:13]:
+        copy.wait()
+    with jax.named_scope("own_latents"):
+        own_latents(core)
+    with jax.named_scope("latent_sum"):
+        next(latents)
 
     f0, f1, f2, f3 = (flags[h] for h in range(4))
     head_of = (
@@ -150,90 +246,8 @@
         f3 + (1 - f3) * 3,
     )
 
-    def own_latents(owner):
-        first = firsts[...].reshape(4 * RANK, WIDTH)
-        for j in range(2):
-            rows = pl.ds(pl.multiple_of(owner * 256 + HALF * j, 256), 256)
-            lat_part = dot(first[: 3 * RANK], xb[rows, :], NT)
-            mix_part = dot(first[3 * RANK :], dob[rows, :], NT)
-            for k in range(2):
-                part[0, owner * 4 + 2 * j + k, : 3 * RANK] = lat_part[:, HD * k : HD * (k + 1)]
-                part[0, owner * 4 + 2 * j + k, 3 * RANK :] = mix_part[:, HD * k : HD * (k + 1)]
-
-    for copy in loads[:6]:
-        copy.wait()
-    with jax.named_scope("own_latents"):
-        own_latents(1 - core)
-    with jax.named_scope("entry_barrier"):
-        pl.semaphore_wait(barrier, len(peers))
-
-    mine = core * 4
-    other = (1 - core) * 4
-
-    def sum_heads(p, late=None):
-        pair = (part.at[p, pl.ds(other, 4)], sib_in.at[p], sib_send.at[p], sib_recv.at[p], sibling)
-        send(*pair)
-        yield
-        remote(*pair).wait_recv()
-        extra = [0.0] * 4 if late is None else late()
-        for i in range(4):
-            acc[p, i] = (part[p, mine + i] + sib_in[p, i] + extra[i]).astype(BF16)
-        shares = [(acc.at[p], y_in.at[p, d - 1], y_send.at[p, d - 1], y_recv.at[p, d - 1], y_peer(d)) for d in range(1, NY)]
-        for share in shares:
-            send(*share)
-        yield
-        for share in shares:
-            remote(*share).wait_recv()
-        for i in range(4):
-            summed = acc[p, i].astype(F32)
-            for d in range(1, NY):
-                summed = summed + y_in[p, d - 1, i].astype(F32)
-            total[p, mine + i] = summed
-        own = total.at[p, pl.ds(mine, 4)]
-        send(own, own, fw_send.at[p], fw_recv.at[p], sibling)
-        yield
-        came = total.at[p, pl.ds(other, 4)]
-        remote(came, came, fw_send.at[p], fw_recv.at[p], sibling).wait_recv()
-        yield
-
-    def sum_tokens(e):
-        for d in range(1, NX):
-            send(cut.at[e, lax.rem(x + d, NX)], x_in.at[e, d - 1], x1_send.at[e, d - 1], x1_recv.at[e, d - 1], x_peer(d))
-        yield
-        summed = cut[e, x].astype(F32)
-        for d in range(1, NX):
-            remote(cut.at[e, 0], x_in.at[e, d - 1], x1_send.at[e, d - 1], x1_recv.at[e, d - 1], x_peer(d)).wait_recv()
-            summed = summed + x_in[e, d - 1].astype(F32)
-        x_sum[e] = summed.astype(BF16)
-        shares = [(x_sum.at[e], z_in.at[e, d - 1], z_send.at[e, d - 1], z_recv.at[e, d - 1], z_peer(d)) for d in range(1, NZ)]
-        for share in shares:
-            send(*share)
-        yield
-        summed = x_sum[e].astype(F32)
-        for d, share in enumerate(shares):
-            remote(*share).wait_recv()
-            summed = summed + z_in[e, d].astype(F32)
-        z_all[e] = summed.astype(BF16)
-        for d in range(1, NX):
-            send(z_all.at[e], x_all.at[e, x], x2_send.at[e, d - 1], x2_recv.at[e, d - 1], x_peer(d))
-        x_all[e, x] = z_all[e]
-        yield
-        for d in range(1, NX):
-            came = x_all.at[e, lax.rem(x + NX - d, NX)]
-            remote(z_all.at[e], came, x2_send.at[e, d - 1], x2_recv.at[e, d - 1], x_peer(d)).wait_recv()
-        for c in range(4):
-            out_ref[e, :, HD * c : HD * (c + 1)] = x_all[e, c].astype(F32)
-        yield
-
-    latents = sum_heads(0)
-    next(latents)
-    with jax.named_scope("own_latents"):
-        own_latents(core)
-    with jax.named_scope("latent_sum"):
-        next(latents)
-
     with jax.named_scope("stage_keys"):
-        for copy in loads[10:18]:
+        for copy in loads[13:21]:
             copy.wait()
         for s in range(2):
             for i, base in enumerate((kb, vb)):
@@ -241,7 +255,7 @@
             send(kv_stage.at[s], kv_in.at[s], kv_send.at[s], kv_recv.at[s], {"ctx": after})
 
     load(*by_head(q_hbm, qb), *by_head(dc_hbm, dcb))
-    for copy in loads[6:10]:
+    for copy in loads[21:25]:
         copy.wait()
     up_pad[...] = jnp.zeros_like(up_pad)
     for t, factor in enumerate(seconds[t] for t in range(4)):
@@ -257,27 +271,27 @@
     with jax.named_scope("latent_sum"):
         next(latents)
 
-    def adapt(i, owner):
-        b = owner * 2 + i % 2 + 4 * (i // 2)
-        rows = pl.ds(pl.multiple_of(b * HD, HD), HD)
-        both = split_rows(2.0 * total[0, owner * 4 + i], 4)
-        lat_low[:, rows] = both.astype(BF16)
-        extra = dot(both.T.astype(BF16), up_pad[...])
-        for t, (base, full, turned) in enumerate(
-            ((qb, qa, None), (kb, ka, kt), (vb, va, vt), (dcb, ua, None))
-        ):
-            for h in range(4):
-                at = WIDTH * t + HD * h
-                low = (base[h, rows, :].astype(F32) + extra[:, at : at + HD]).astype(BF16)
-                full[h, rows, :] = low
-                if turned is not None:
-                    turned[h, :, rows] = low.T
-        return owner
-
-    for copy in loads[18:]:
+    def adapt(owner):
+        for j in range(2):
+            rows = rows_of(owner, j)
+            both = jnp.concatenate([split_rows(2.0 * total[0, owner * 4 + 2 * j + k], 4) for k in range(2)], axis=1)
+            lat_low[:, rows] = both.astype(BF16)
+            cols = both.T.astype(BF16)
+            for t, (base, full, turned) in enumerate(
+                ((kb, ka, kt), (vb, va, vt), (qb, qa, None), (dcb, ua, None))
+            ):
+                kind = (1, 2, 0, 3)[t]
+                extra = dot(cols, up_pad[:, WIDTH * kind : WIDTH * (kind + 1)])
+                for h in range(4):
+                    low = (base[h, rows, :].astype(F32) + extra[:, HD * h : HD * (h + 1)]).astype(BF16)
+                    full[h, rows, :] = low
+                    if turned is not None:
+                        turned[h, :, rows] = low.T
+
+    for copy in loads[25:]:
         copy.wait()
     with jax.named_scope("adapt"):
-        lax.fori_loop(0, 4, adapt, core)
+        adapt(core)
     with jax.named_scope("latent_sum"):
         next(latents)
     for c in range(2):
@@ -286,16 +300,7 @@
             lp_send.at[c], lp_recv.at[c], {"ctx": after},
         )
     with jax.named_scope("adapt"):
-        lax.fori_loop(0, 4, adapt, 1 - core)
-        for c in range(2):
-            remote(
-                total.at[0, pl.ds(4 * c + 2, 2), pl.ds(RANK, 2 * RANK)], lat_prev.at[pl.ds(2 * c, 2)],
-                lp_send.at[c], lp_recv.at[c], {"ctx": after},
-            ).wait_recv()
-        for b in range(4):
-            both = split_rows(2.0 * lat_prev[b], 2)
-            prev_low[:, HD * b : HD * (b + 1)] = both.astype(BF16)
-            prev_cols[HD * b : HD * (b + 1), :] = both.T.astype(BF16)
+        adapt(1 - core)
 
     def chunk(j, slot, at, with_off, c, sums):
         h = head_of[slot]
@@ -415,7 +420,20 @@
             {"ctx": before, "head": y * 2 + c},
         )
 
+    def latents_from_before():
+        for c in range(2):
+            remote(
+                total.at[0, pl.ds(4 * c + 2, 2), pl.ds(RANK, 2 * RANK)], lat_prev.at[pl.ds(2 * c, 2)],
+                lp_send.at[c], lp_recv.at[c], {"ctx": after},
+            ).wait_recv()
+        for b in range(4):
+            both = split_rows(2.0 * lat_prev[b], 2)
+            prev_low[:, HD * b : HD * (b + 1)] = both.astype(BF16)
+            prev_cols[HD * b : HD * (b + 1), :] = both.T.astype(BF16)
+
     def keys_from_before(slot):
+        if slot == 0:
+            latents_from_before()
         remote(
             kv_stage.at[slot], kv_in.at[slot], kv_send.at[slot], kv_recv.at[slot], {"ctx": after}
         ).wait_recv()
@@ -436,15 +454,15 @@
     with jax.named_scope("attend"):
         chunks, at_start, at_end, shares = [], {}, {}, []
         all_sums = [{}, {}, {}, {}]
-        order = [(0, False), (1, False), (0, True), (1, True), (2, False), (2, True), (3, False), (3, True)]
+        order = [(0, False), (1, False), (2, False), (2, True), (0, True), (1, True), (3, True), (3, False)]
         for slot, with_off in order:
             first_at = HALF if slot < 2 else 0
             if slot < 2 and with_off:
                 at_start[len(chunks)] = functools.partial(keys_from_before, slot)
-            for c in range(2):
+            for c in ((1, 0) if (slot, with_off) == (3, False) else (0, 1)):
                 at = HALF - first_at if with_off else first_at
                 chunks.append(chunk(len(chunks), slot, at, with_off, c, all_sums[slot]))
-            if with_off:
+            if with_off != (slot == 3):
                 at_end[len(chunks) - 1] = functools.partial(keys_done, slot, all_sums[slot])
         count = len(chunks)
         for step in chunks[0][0]:
@@ -459,11 +477,11 @@
                 step()
             if j - 1 in at_end:
                 at_end[j - 1]()
-            if j - 1 == 7:
+            if j - 1 == 11:
                 send_back()
             if j == count - 1:
-                shares = projections((0, 1))
-        wide = jnp.concatenate([a + b for a, b in zip(shares, projections((2, 3)))], axis=0)
+                shares = [a + b for a, b in zip(projections((0, 1)), projections((2,)))]
+        wide = jnp.concatenate([a + b for a, b in zip(shares, projections((3,)))], axis=0)
 
     with jax.named_scope("share_sum"):
         for b in range(8):
@@ -479,14 +497,16 @@
 
         shares = sum_heads(1, add_back)
         next(shares)
-        next(shares)
         every = (0, 1, 2, 3)
         up_rows = [
-            fold(dot(lat_low[:32, :], stacked(grad_q, every), NT)),
+            None,
             fold(dot(lat_low[32:64, :], beside(grad_k, every))),
             fold(dot(lat_low[64:96, :], beside(grad_v, every))),
-            fold(dot(lat_low[96:, :], stacked(ctx_all, every), NT)),
+            None,
         ]
+        next(shares)
+        up_rows[0] = fold(dot(lat_low[:32, :], stacked(grad_q, every), NT))
+        up_rows[3] = fold(dot(lat_low[96:, :], stacked(ctx_all, every), NT))
         for t, ref in ((1, back_k), (2, back_v)):
             extra = fold(dot(prev_low[32 * t - 32 : 32 * t, :], beside(ref, (0, 1))))
             up_rows[t] = up_rows[t] + jnp.concatenate([extra, jnp.zeros_like(extra)], axis=1)
@@ -505,7 +525,7 @@
         down = jnp.zeros((96, WIDTH), F32)
         last = jnp.zeros((32, WIDTH), F32)
         for j in range(2):
-            rows = pl.ds(pl.multiple_of(owner * 256 + HALF * j, 256), 256)
+            rows = rows_of(owner, j)
             here = wide[:, 256 * j : 256 * (j + 1)]
             down = down + dot(here[:96], xb[rows, :])
             last = last + dot(here[96:], dob[rows, :])
@@ -520,10 +540,10 @@
     with jax.named_scope("token_sum"):
         downs = sum_tokens(1)
         next(downs)
+        next(downs)
         next(ups)
         next(downs)
         next(ups)
-        next(downs)
         next(downs)
     for copy in sends:
         copy.wait_send()
@@ -537,16 +557,15 @@
 ):
     anywhere = pl.BlockSpec(memory_space=pl.ANY)
     vmem = pl.BlockSpec(memory_space=pltpu.VMEM)
-    smem = pl.BlockSpec(memory_space=pltpu.SMEM)
     dma = pltpu.SemaphoreType.DMA
     v = pltpu.VMEM
     out = pl.pallas_call(
         kernel,
-        out_shape=jax.ShapeDtypeStruct((2, 64, WIDTH), F32),
-        in_specs=[anywhere] * 6 + [smem] + [anywhere] * 8,
+        out_shape=pltpu.VMEM((2, 64, WIDTH), F32),
+        in_specs=[anywhere] * 15,
         out_specs=vmem,
         scratch_shapes=[
-            v((4, RANK, WIDTH), BF16), v((4, RANK, WIDTH), BF16),
+            pltpu.SMEM((4,), jnp.int32), v((4, RANK, WIDTH), BF16), v((4, RANK, WIDTH), BF16),
             v((ROWS, WIDTH), BF16), *[v((4, ROWS, HD), BF16) for _ in range(3)],
             v((ROWS, WIDTH), BF16), v((4, ROWS, HD), BF16),
             v((2, 2, HALF, HD), BF16), v((2, 2, HALF, HD), BF16),
@@ -563,7 +582,7 @@
             v((2, 2, 32, HD), F32), v((2, 2, 32, HD), F32), v((4, 64, HD), F32),
             v((2, 4, 64, HD), BF16), v((2, 3, 64, HD), BF16), v((2, 64, HD), BF16),
             v((2, 7, 64, HD), BF16), v((2, 64, HD), BF16), v((2, 4, 64, HD), BF16),
-            dma((26,)), dma((2,)), dma((2,)), dma((2,)), dma((2,)), dma((2,)), dma((2,)),
+            dma((33,)), dma((2,)), dma((2,)), dma((2,)), dma((2,)), dma((2,)), dma((2,)),
             dma((2,)), dma((2,)), dma((2, 3)), dma((2, 3)), dma((2,)), dma((2,)),
             dma((2, 3)), dma((2, 3)), dma((2, 7)), dma((2, 7)), dma((2, 3)), dma((2, 3)),
         ],

time: 64.1 us -> 56.7 us (0.88)
  Pallas kernels: 61.7 us -> 55.2 us
  local copies, waits for them, and re-layouts: 1.57 us -> 0.7 us
    pallas_call x1, Pallas kernels: 61.7 us -> 55.2 us  [on_device(): pl.pallas_call(kernel, out_shape=pltpu.VMEM((2, 64, WIDTH), F32), in_spec...]
    squeeze x1, local copies, waits for them, and re-layouts: 1.57 us -> 0.7 us  [on_device(): result += [out[1, rows], out[0, rows]]]
where the time goes in v4:
time: 56.7 us; the launch traced here: 56.5 us
  Pallas kernels  55.2 us (97%)
  local copies, waits for them, and re-layouts  0.7 us (1%)
  between operations  0.65 us (1%)
    pallas_call x1, Pallas kernels, on_device(): pl.pallas_call(kernel, out_shape=pltpu.VMEM((2, 64, WIDTH), F32), in_spec...  55.2 us

profile of v4, /device:TPU:1, one launch (start us, length us, event | category | flops | bytes accessed | tf_op | source)
XLA Modules:
  0.0 56.5 jit_solution(1783202212411401067)
XLA Ops:
  0.6 55.2 %shard_map.206 = f32[2,64,512]{2,1,0:T(8,128)S(1)} custom-call(bf16[1024,512]{1,0:T(8,128)(2,1)} %bitcast.22, bf16[1024,512]{1,0:T(8,128)(2,1)} %bitcast.23, bf16[1024,512]{1,0:T(8,128)(2,1)} %bitcast.24, bf16[1024,512]{1,0:T(8,128)(2,1)} %bitcast.25, bf16[1024,512]{1,0:T(8,128)(2,1)} %bitcast.26, bf16[1024,512]{1,0:T(8,128)(2,1)} %bitcast.27, s32[4]{0:T(128)} %flags_hbm.1, ...), custom_call_target="tpu_custom_call" | custom-call | tf_op jit(solution)/shard_map/pallas_call | solution.py:562
  55.8 0.7 %slice_bitcast_fusion = (f32[16,512]{1,0:T(8,128)}, f32[16,512]{1,0:T(8,128)}, f32[16,512]{1,0:T(8,128)}, f32[16,512]{1,0:T(8,128)}, f32[16,512]{1,0:T(8,128)}, ...) fusion(f32[2,64,512]{2,1,0:T(8,128)S(1)} %shard_map.206), kind=kLoop, calls=%fused_computation | loop fusion | bytes 524288 | tf_op jit(solution)/shard_map/squeeze | solution.py:599

commit v5 on v4

--- a/solution.py
+++ b/solution.py
@@ -117,7 +117,7 @@
 
     load(
         (down_q_hbm, firsts.at[0]), (down_k_hbm, firsts.at[1]), (down_v_hbm, firsts.at[2]), (up_o_hbm, firsts.at[3]),
-        *by_owner(1 - core), *by_owner(core), (flags_hbm, flags),
+        *by_owner(1 - core), *by_owner(core), (flags_hbm, flags), *by_head(k_hbm, kb), *by_head(v_hbm, vb),
     )
 
     barrier = pltpu.get_barrier_semaphore()
@@ -222,15 +222,12 @@
     latents = sum_heads(0)
     next(latents)
     load(
-        *by_head(k_hbm, kb), *by_head(v_hbm, vb),
         (up_q_hbm, seconds.at[0]), (up_k_hbm, seconds.at[1]), (up_v_hbm, seconds.at[2]), (down_o_hbm, seconds.at[3]),
     )
     for copy in loads[8:13]:
         copy.wait()
     with jax.named_scope("own_latents"):
         own_latents(core)
-    with jax.named_scope("latent_sum"):
-        next(latents)
 
     f0, f1, f2, f3 = (flags[h] for h in range(4))
     head_of = (
@@ -246,13 +243,17 @@
         f3 + (1 - f3) * 3,
     )
 
+    def stage_keys(slot):
+        for i, base in enumerate((kb, vb)):
+            kv_stage[slot, i] = base[head_of[slot], HALF:, :]
+        send(kv_stage.at[slot], kv_in.at[slot], kv_send.at[slot], kv_recv.at[slot], {"ctx": after})
+
+    for copy in loads[13:21]:
+        copy.wait()
     with jax.named_scope("stage_keys"):
-        for copy in loads[13:21]:
-            copy.wait()
-        for s in range(2):
-            for i, base in enumerate((kb, vb)):
-                kv_stage[s, i] = base[head_of[s], HALF:, :]
-            send(kv_stage.at[s], kv_in.at[s], kv_send.at[s], kv_recv.at[s], {"ctx": after})
+        stage_keys(0)
+    with jax.named_scope("latent_sum"):
+        next(latents)
 
     load(*by_head(q_hbm, qb), *by_head(dc_hbm, dcb))
     for copy in loads[21:25]:
@@ -299,6 +300,8 @@
             total.at[0, pl.ds(4 * c + 2, 2), pl.ds(RANK, 2 * RANK)], lat_prev.at[pl.ds(2 * c, 2)],
             lp_send.at[c], lp_recv.at[c], {"ctx": after},
         )
+    with jax.named_scope("stage_keys"):
+        stage_keys(1)
     with jax.named_scope("adapt"):
         adapt(1 - core)
 
@@ -454,7 +457,7 @@
     with jax.named_scope("attend"):
         chunks, at_start, at_end, shares = [], {}, {}, []
         all_sums = [{}, {}, {}, {}]
-        order = [(0, False), (1, False), (2, False), (2, True), (0, True), (1, True), (3, True), (3, False)]
+        order = [(0, False), (1, False), (2, False), (2, True), (0, True), (3, True), (1, True), (3, False)]
         for slot, with_off in order:
             first_at = HALF if slot < 2 else 0
             if slot < 2 and with_off:
@@ -477,7 +480,7 @@
                 step()
             if j - 1 in at_end:
                 at_end[j - 1]()
-            if j - 1 == 11:
+            if j - 1 == 13:
                 send_back()
             if j == count - 1:
                 shares = [a + b for a, b in zip(projections((0, 1)), projections((2,)))]

time: 56.7 us -> 54.2 us (0.956)
  Pallas kernels: 55.2 us -> 52.7 us
    pallas_call x1, Pallas kernels: 55.2 us -> 52.7 us  [on_device(): pl.pallas_call(kernel, out_shape=pltpu.VMEM((2, 64, WIDTH), F32), in_spec...]
where the time goes in v5:
time: 54.2 us; the launch traced here: 54.1 us
  Pallas kernels  52.7 us (97%)
  local copies, waits for them, and re-layouts  0.7 us (1%)
  between operations  0.65 us (1%)
    pallas_call x1, Pallas kernels, on_device(): pl.pallas_call(kernel, out_shape=pltpu.VMEM((2, 64, WIDTH), F32), in_spec...  52.7 us

profile of v5, /device:TPU:1, one launch (start us, length us, event | category | flops | bytes accessed | tf_op | source)
XLA Modules:
  0.0 54.1 jit_solution(17162317566013599804)
XLA Ops:
  0.6 52.7 %shard_map.206 = f32[2,64,512]{2,1,0:T(8,128)S(1)} custom-call(bf16[1024,512]{1,0:T(8,128)(2,1)} %bitcast.22, bf16[1024,512]{1,0:T(8,128)(2,1)} %bitcast.23, bf16[1024,512]{1,0:T(8,128)(2,1)} %bitcast.24, bf16[1024,512]{1,0:T(8,128)(2,1)} %bitcast.25, bf16[1024,512]{1,0:T(8,128)(2,1)} %bitcast.26, bf16[1024,512]{1,0:T(8,128)(2,1)} %bitcast.27, s32[4]{0:T(128)} %flags_hbm.1, ...), custom_call_target="tpu_custom_call" | custom-call | tf_op jit(solution)/shard_map/pallas_call | solution.py:565
  53.4 0.7 %slice_bitcast_fusion = (f32[16,512]{1,0:T(8,128)}, f32[16,512]{1,0:T(8,128)}, f32[16,512]{1,0:T(8,128)}, f32[16,512]{1,0:T(8,128)}, f32[16,512]{1,0:T(8,128)}, ...) fusion(f32[2,64,512]{2,1,0:T(8,128)S(1)} %shard_map.206), kind=kLoop, calls=%fused_computation | loop fusion | bytes 524288 | tf_op jit(solution)/shard_map/squeeze | solution.py:602

commit v6 on v5

--- a/solution.py
+++ b/solution.py
@@ -289,19 +289,19 @@
                     if turned is not None:
                         turned[h, :, rows] = low.T
 
+    for c in range(2):
+        send(
+            total.at[0, pl.ds(mine + 2, 2), pl.ds(RANK, 2 * RANK)], lat_prev.at[pl.ds(2 * core, 2)],
+            lp_send.at[c], lp_recv.at[core], {"ctx": after, "head": y * 2 + c},
+        )
+    with jax.named_scope("stage_keys"):
+        stage_keys(1)
     for copy in loads[25:]:
         copy.wait()
     with jax.named_scope("adapt"):
         adapt(core)
     with jax.named_scope("latent_sum"):
         next(latents)
-    for c in range(2):
-        send(
-            total.at[0, pl.ds(4 * c + 2, 2), pl.ds(RANK, 2 * RANK)], lat_prev.at[pl.ds(2 * c, 2)],
-            lp_send.at[c], lp_recv.at[c], {"ctx": after},
-        )
-    with jax.named_scope("stage_keys"):
-        stage_keys(1)
     with jax.named_scope("adapt"):
         adapt(1 - core)
 

time: 54.2 us -> 53.2 us (0.982)
  Pallas kernels: 52.7 us -> 51.7 us
    pallas_call x1, Pallas kernels: 52.7 us -> 51.7 us  [on_device(): pl.pallas_call(kernel, out_shape=pltpu.VMEM((2, 64, WIDTH), F32), in_spec...]
where the time goes in v6:
time: 53.2 us; the launch traced here: 53 us
  Pallas kernels  51.7 us (97%)
  local copies, waits for them, and re-layouts  0.7 us (1%)
  between operations  0.65 us (1%)
    pallas_call x1, Pallas kernels, on_device(): pl.pallas_call(kernel, out_shape=pltpu.VMEM((2, 64, WIDTH), F32), in_spec...  51.7 us

profile of v6, /device:TPU:1, one launch (start us, length us, event | category | flops | bytes accessed | tf_op | source)
XLA Modules:
  0.0 53.0 jit_solution(9918555898797321983)
XLA Ops:
  0.6 51.7 %shard_map.206 = f32[2,64,512]{2,1,0:T(8,128)S(1)} custom-call(bf16[1024,512]{1,0:T(8,128)(2,1)} %bitcast.22, bf16[1024,512]{1,0:T(8,128)(2,1)} %bitcast.23, bf16[1024,512]{1,0:T(8,128)(2,1)} %bitcast.24, bf16[1024,512]{1,0:T(8,128)(2,1)} %bitcast.25, bf16[1024,512]{1,0:T(8,128)(2,1)} %bitcast.26, bf16[1024,512]{1,0:T(8,128)(2,1)} %bitcast.27, s32[4]{0:T(128)} %flags_hbm.1, ...), custom_call_target="tpu_custom_call" | custom-call | tf_op jit(solution)/shard_map/pallas_call | solution.py:565
  52.3 0.7 %slice_bitcast_fusion = (f32[16,512]{1,0:T(8,128)}, f32[16,512]{1,0:T(8,128)}, f32[16,512]{1,0:T(8,128)}, f32[16,512]{1,0:T(8,128)}, f32[16,512]{1,0:T(8,128)}, ...) fusion(f32[2,64,512]{2,1,0:T(8,128)S(1)} %shard_map.206), kind=kLoop, calls=%fused_computation | loop fusion | bytes 524288 | tf_op jit(solution)/shard_map/squeeze | solution.py:602
